TPU v7x, 512 devices: a whole 4x4x16 slice. The times are simulated.
512 devices in a mesh: seq: 128 (over z, x, core), row: 2 (over y_hi), col: 2 (over y_lo).
Axes of the slice: x: 4, y: 4 (y_hi: 2, y_lo: 2; y = y_hi * 2 + y_lo), z: 16, core: 2. Of those that a mesh axis runs over, the one named last changes fastest.
Arguments:
- atom_single: bfloat16 [16384, 128], P('seq'), may hold values from -6 to 6
- token_single: bfloat16 [2048, 384], P('seq', 'row'), may hold values from -6 to 6
- pair_band: bfloat16 [2048, 80, 128], P(('seq', 'row'), 'col'), may hold values from -6 to 6
- token_counts: int32 [2048], P('seq'), may hold values from 1 to 23, as said below
- atom_token: int32 [16384], P('seq'), may hold values from 0 to 2047, as said below
- window_starts: int32 [512], P('seq'), may hold values from 0 to 16256, as said below
- single_proj: bfloat16 [384, 128], P('row'), may hold values from -0.3125 to 0.3125
- pair_proj: float32 [128, 12], replicated, may hold values from -6 to 6
- attn_in: bfloat16 [3, 128, 512], replicated, may hold values from -0.5 to 0.5
- attn_out: bfloat16 [3, 128, 128], replicated, may hold values from -0.5 to 0.5
- trans_in: bfloat16 [3, 128, 512], replicated, may hold values from -0.5 to 0.5
- trans_out: bfloat16 [3, 256, 128], replicated, may hold values from -0.375 to 0.375
- agg_proj: bfloat16 [128, 768], P(None, 'row'), may hold values from -0.5 to 0.5
- token_cot: bfloat16 [2048, 768], P('seq', 'row'), may hold values from -6 to 6
Outputs:
- token_act: bfloat16 [2048, 768], P('seq', 'row')
- atom_grad: bfloat16 [16384, 128], P('seq')
- single_grad: bfloat16 [2048, 384], P('seq', 'row')
Inputs may be any that keep to these rules, and one draw needn't show every extreme that they name: `token_counts`: the counts of each aligned block of 16 tokens sum to 128 plus a difference of drifts: the first atom of the tokens of block j lies within 32 atoms of atom 8 * 16 * j, and that distance occurs in every draw. Tokens 2k and 2k + 1 together own at least 8 atoms, exactly 8 in some pair of every draw. `atom_token`: atoms are ordered by token: token t owns token_counts[t] consecutive atoms. `window_starts`: the window of query block b starts between 64 and 32 atoms before its first atom, clipped to the atoms; both ends occur in every draw.
All inputs are finite; a program needn't handle non-finite values.
Results may differ from a plain program's by a relative error of at most 0.015.
The roundings to bfloat16 on the way count: a program that leaves them out, or rounds other values in their place, can miss the bound.
Values may be sent and summed in bfloat16 or wider, within the bound.
A program may use at most 128 MiB of HBM per device.

v0:
```python
import functools

import jax
import jax.numpy as jnp
from jax import lax
from jax.experimental import pallas as pl
from jax.experimental.pallas import tpu as pltpu
from jax.sharding import PartitionSpec as P

HEADS = 4
QB = 32
KW = 128
LAYERS = 3
ATOMS = 128
CA = 128
TOK = 16
COND = 192
ACT = 384
FFA = 256
PAIR_ROWS = 8
PAIR_COLS = 40
PAIR_PAD = 48
SPAN = 3 * TOK
HALF = 64
EXT = 256
ALL = HEADS * ATOMS
F32 = jnp.float32
BF16 = jnp.bfloat16
EPS = 1e-05
SCALE = (CA // HEADS) ** (-0.5)
MESH = pl.DeviceIdType.MESH

PARTNERS = [
    (ds, dr, dc)
    for ds in (0, -1, 1)
    for dr in (0, 1)
    for dc in (0, 1)
    if (ds, dr, dc) != (0, 0, 0)
]
COND_PARTNERS = [p for p in PARTNERS if p[2] == 0]
SIDES = (-1, 1)


def nn(a, b):
    return lax.dot_general(a, b, (((1,), (0,)), ((), ())), preferred_element_type=F32)


def nt(a, b):
    return lax.dot_general(a, b, (((1,), (1,)), ((), ())), preferred_element_type=F32)


def flip(values):
    return jnp.transpose(values, (1, 0))


def iota(shape, dim):
    return lax.broadcasted_iota(jnp.int32, shape, dim)


def norm_rows(values):
    centre = values - jnp.mean(values, axis=0, keepdims=True)
    scaling = lax.rsqrt(jnp.mean(centre * centre, axis=0, keepdims=True) + EPS)
    return centre * scaling, scaling


def norm_back(normal, scaling, upstream):
    return scaling * (
        upstream
        - jnp.mean(upstream, axis=0, keepdims=True)
        - normal * jnp.mean(upstream * normal, axis=0, keepdims=True)
    )


def by_head(rows):
    head = iota(rows.shape, 1) // (CA // HEADS)
    return jnp.concatenate(
        [jnp.where(head == h, rows, 0.0).astype(BF16) for h in range(HEADS)], axis=0
    )


def split(values):
    high = values.astype(BF16)
    return high, (values - high.astype(F32)).astype(BF16)


def kernel(
    atom_ref,
    single_ref,
    band_ref,
    counts_ref,
    ids_ref,
    starts_ref,
    proj_ref,
    pair_proj_ref,
    attn_in_ref,
    attn_out_ref,
    trans_in_ref,
    trans_out_ref,
    agg_ref,
    cot_ref,
    act_out,
    grad_out,
    single_out,
    id_buf,
    halo_buf,
    cond_buf,
    pair_buf,
    cot_buf,
    agg_buf,
    kv,
    bias,
    mixed,
    gate_t,
    out_t,
    in_t,
    down_t,
    soft,
    soft_b,
    q_heads,
    key_t,
    normal_x,
    scale_x,
    normal_m,
    scale_m,
    gating,
    gate_back,
    silu_a,
    back_a,
    dkv_send,
    dkv_recv,
    sums_send,
    sums_recv,
    cond_send,
    cond_recv,
    send_sem,
    recv_sem,
):
    seq = lax.axis_index("seq")
    row = lax.axis_index("row")
    col = lax.axis_index("col")
    seqs = lax.axis_size("seq")

    def partner(ds, dr, dc):
        return (
            lax.rem(seq + ds + seqs, seqs),
            lax.rem(row + dr, 2),
            lax.rem(col + dc, 2),
        )

    copies = []

    def send(src, dst, ds, dr=0, dc=0):
        place = len(copies)
        copy = pltpu.make_async_remote_copy(
            src_ref=src,
            dst_ref=dst,
            send_sem=send_sem.at[place],
            recv_sem=recv_sem.at[place],
            device_id=partner(ds, dr, dc),
            device_id_type=MESH,
        )
        copy.start()
        copies.append(copy)
        return copy

    barrier = pltpu.get_barrier_semaphore()
    for ds, dr, dc in PARTNERS:
        pl.semaphore_signal(barrier, inc=1, device_id=partner(ds, dr, dc), device_id_type=MESH)

    cond_buf[1, 0] = nn(single_ref[...], proj_ref[...])
    place_h = (iota((LAYERS * HEADS, CA), 1) == 8 * iota((LAYERS * HEADS, CA), 0)).astype(BF16)
    pp_high, pp_rest = split(pair_proj_ref[...])
    spread_high = nn(pp_high, place_h).astype(BF16)
    spread_rest = nn(pp_rest, place_h).astype(BF16)
    band = band_ref[...].astype(F32).reshape(PAIR_ROWS * PAIR_COLS, CA)
    centre = band - jnp.mean(band, axis=1, keepdims=True)
    normal = centre * lax.rsqrt(jnp.mean(centre * centre, axis=1, keepdims=True) + EPS)
    n_high, n_rest = split(normal)
    pairs = nn(n_high, spread_high) + nn(n_high, spread_rest) + nn(n_rest, spread_high)
    tile = pairs[:PAIR_COLS]
    for i in range(1, PAIR_ROWS):
        tile = tile + pltpu.roll(pairs[PAIR_COLS * i : PAIR_COLS * (i + 1)], i, 1)
    tile = jnp.concatenate([tile, jnp.zeros((PAIR_PAD - PAIR_COLS, CA), F32)], axis=0)
    pair_rows = pl.ds(pl.multiple_of(col * PAIR_PAD, 16), PAIR_PAD)
    pair_lanes = pl.ds(pl.multiple_of(row * CA, CA), CA)
    pair_buf[1, pair_rows, pair_lanes] = tile.astype(BF16)
    cot_buf[1, 0] = cot_ref[...]

    pl.semaphore_wait(barrier, len(PARTNERS))

    cond_copies = [
        send(cond_buf.at[1, 0], cond_buf.at[1 - ds, dr], ds, dr) for ds, dr, dc in COND_PARTNERS
    ]
    id_copies = [send(ids_ref, id_buf.at[1 - ds], ds) for ds in SIDES]
    halo_copies = [
        send(atom_ref.at[pl.ds(0, HALF)], halo_buf.at[pl.ds(0, HALF)], -1),
        send(atom_ref.at[pl.ds(HALF, HALF)], halo_buf.at[pl.ds(HALF, HALF)], 1),
    ]
    pair_copies = [
        send(
            pair_buf.at[1, pair_rows, pair_lanes],
            pair_buf.at[1 - ds, pair_rows, pair_lanes],
            ds,
            dr,
            dc,
        )
        for ds, dr, dc in PARTNERS
    ]
    cot_copies = [
        send(cot_buf.at[1, 0], cot_buf.at[1 - ds, dr], ds, dr) for ds, dr, dc in COND_PARTNERS
    ]
    agg_copy = send(agg_ref, agg_buf, 0, 1)

    for n in range(LAYERS):
        gate_t[n] = flip(attn_in_ref[n, :, 3 * CA :])
        out_t[n] = flip(attn_out_ref[n])
        in_t[n] = flip(trans_in_ref[n])
        down_t[n] = flip(trans_out_ref[n])

    token_base = TOK * (seq - 1)
    own_ids = ids_ref[...] - token_base
    own_id_cols = flip(jnp.broadcast_to(own_ids.astype(F32), (CA, ATOMS))).astype(jnp.int32)
    atom_t = flip(atom_ref[...].astype(F32))
    low = iota((1, ATOMS), 1) < HALF

    for copy in id_copies + halo_copies + cond_copies:
        copy.wait_recv()
    halo_ids = jnp.where(low, id_buf[2], id_buf[0]) - token_base
    halo_id_cols = flip(jnp.broadcast_to(halo_ids.astype(F32), (CA, ATOMS))).astype(jnp.int32)
    id_rows = jnp.concatenate([own_ids, halo_ids], axis=1)
    id_cols = jnp.concatenate([own_id_cols, halo_id_cols], axis=0)
    pick_ext = (iota((SPAN, EXT), 0) == id_rows).astype(F32).astype(BF16)
    pick = pick_ext[:, :ATOMS]
    at_token = id_cols == iota((EXT, CA), 1)
    pick_t = at_token[:ATOMS].astype(F32).astype(BF16)[:, :SPAN]
    token_atoms = jnp.sum(at_token.astype(F32), axis=0, keepdims=True)
    atom_counts = jnp.sum(
        jnp.where(at_token[:ATOMS], token_atoms, 0.0), axis=1, keepdims=True
    )
    inverse = 1.0 / jnp.maximum(atom_counts, 1.0)
    cond = (cond_buf[:, 0] + cond_buf[:, 1]).astype(BF16).reshape(SPAN, CA)
    cond_t = flip(cond.astype(F32)).astype(BF16)
    stream_ext = jnp.concatenate([atom_t, flip(halo_buf[...].astype(F32))], axis=1) + nn(
        cond_t, pick_ext
    )

    position = iota((EXT, ATOMS), 0)
    position = jnp.where(position < ATOMS + HALF, position, position - EXT)
    lane = iota((1, ATOMS), 1)
    first = jnp.zeros((1, ATOMS), jnp.int32)
    for b in range(ATOMS // QB):
        first = jnp.where(lane // QB == b, starts_ref[b] - seq * ATOMS, first)
    inside = (position >= first) & (position < first + KW)
    outside = jnp.where(inside, 0.0, -1e30)
    outside = jnp.concatenate([outside] * HEADS, axis=1)

    def bias_mixed():
        lanes = iota((EXT, 2 * PAIR_PAD), 1)
        column = jnp.where(
            lanes < PAIR_PAD,
            jnp.where(lanes < PAIR_COLS, lanes, -4096),
            jnp.where(lanes < PAIR_PAD + PAIR_COLS, lanes - (PAIR_PAD - PAIR_COLS), -4096),
        )
        for s in range(3):
            take = (id_cols[:, : 2 * PAIR_PAD] + (2 - s) * TOK == column).astype(F32).astype(BF16)
            mixed[:, 2 * CA * s : 2 * CA * (s + 1)] = nn(take, pair_buf[s]).astype(BF16)

    wide = 3 * 2 * CA
    place = iota((wide, ATOMS), 0)
    head_of = (place // PAIR_ROWS) % (CA // PAIR_ROWS)
    token_of = TOK * (place // (2 * CA)) + PAIR_ROWS * ((place // CA) % 2) + place % PAIR_ROWS
    token_hit = token_of == own_ids

    def bias_layer(n):
        picks = jnp.concatenate(
            [
                (token_hit & (head_of == HEADS * n + h)).astype(F32).astype(BF16)
                for h in range(HEADS)
            ],
            axis=1,
        )
        bias[n] = nn(mixed[...], picks) + outside

    stream = stream_ext[:, :ATOMS]
    for n in range(LAYERS):
        wait_for = []
        if n == 0:
            normal_ext, scale_ext = norm_rows(stream_ext)
            normal_x[n] = normal_ext[:, :ATOMS]
            scale_x[n] = scale_ext[:, :ATOMS]
            normed = normal_ext[:, :ATOMS].astype(BF16)
            rows_ext = flip(normal_ext).astype(BF16)
            rows = rows_ext[:ATOMS]
            kv[n] = nn(rows_ext, attn_in_ref[n, :, CA : 3 * CA]).astype(BF16)
        else:
            normal, scaling = norm_rows(stream)
            normal_x[n] = normal
            scale_x[n] = scaling
            normed = normal.astype(BF16)
            rows = flip(normal).astype(BF16)
            kv[n, :ATOMS] = nn(rows, attn_in_ref[n, :, CA : 3 * CA]).astype(BF16)
            wait_for = [
                send(kv.at[n, pl.ds(0, HALF)], kv.at[n, pl.ds(ATOMS, HALF)], -1),
                send(kv.at[n, pl.ds(HALF, HALF)], kv.at[n, pl.ds(ATOMS + HALF, HALF)], 1),
            ]
        queries = nn(rows, attn_in_ref[n, :, :CA]).astype(BF16).astype(F32)
        q_heads[n] = by_head(queries)
        gates = jax.nn.sigmoid(nn(gate_t[n], normed))
        if n == 0:
            for copy in pair_copies:
                copy.wait_recv()
            bias_mixed()
        bias_layer(n)
        own_scores = nt(kv[n, :ATOMS, :CA], q_heads[n]) * SCALE + bias[n, :ATOMS]
        own_values = flip(kv[n, :ATOMS, CA:])
        for copy in wait_for:
            copy.wait_recv()
        halo_scores = nt(kv[n, ATOMS:, :CA], q_heads[n]) * SCALE + bias[n, ATOMS:]
        halo_values = flip(kv[n, ATOMS:, CA:])
        most = jnp.maximum(
            jnp.max(own_scores, axis=0, keepdims=True), jnp.max(halo_scores, axis=0, keepdims=True)
        )
        own_exp = jnp.exp(own_scores - most)
        halo_exp = jnp.exp(halo_scores - most)
        total = jnp.sum(own_exp, axis=0, keepdims=True) + jnp.sum(halo_exp, axis=0, keepdims=True)
        share = 1.0 / total
        own_soft = own_exp * share
        halo_soft = halo_exp * share
        soft[n, :ATOMS] = own_soft
        soft[n, ATOMS:] = halo_soft
        soft_b[n, :ATOMS] = own_soft.astype(BF16)
        soft_b[n, ATOMS:] = halo_soft.astype(BF16)
        values_t = jnp.concatenate([own_values, halo_values], axis=1)
        width = CA // HEADS
        attended = jnp.concatenate(
            [
                nn(
                    values_t[width * h : width * (h + 1)],
                    soft_b[n, :, ATOMS * h : ATOMS * (h + 1)],
                )
                for h in range(HEADS)
            ],
            axis=0,
        )
        gated = gates * attended
        gating[n] = gates
        gate_back[n] = gated * (1.0 - gates)
        x_mid = stream + nn(out_t[n], gated.astype(BF16))
        normal, scaling = norm_rows(x_mid)
        normal_m[n] = normal
        scale_m[n] = scaling
        widened = nn(in_t[n], normal.astype(BF16))
        part_a = widened[:FFA]
        part_b = widened[FFA:]
        sig = jax.nn.sigmoid(part_a)
        act = part_a * sig
        silu_a[n] = act
        back_a[n] = part_b * (sig * (1.0 + part_a * (1.0 - sig)))
        stream = x_mid + nn(down_t[n], (act * part_b).astype(BF16))
        key_t[n, :, :ATOMS] = flip(kv[n, :ATOMS, :CA])
        key_t[n, :, ATOMS:] = flip(kv[n, ATOMS:, :CA])

    final = flip(stream).astype(BF16)
    agg_copy.wait_recv()
    for copy in cot_copies:
        copy.wait_recv()
    gradient = None
    for part in range(2):
        weights = agg_ref[...] if part == 0 else agg_buf[...]
        pre = nn(final, weights)
        sig = jax.nn.sigmoid(pre)
        d_act = nn(pick_t, cot_buf[:, part].reshape(SPAN, ACT)) * inverse
        d_pre = (d_act * (sig * (1.0 + pre * (1.0 - sig)))).astype(BF16)
        term = nt(weights, d_pre)
        gradient = term if part == 0 else gradient + term
        if part == 0:
            high, rest = split(pre * sig)
            sums = nn(pick, high) + nn(pick, rest)
            sums_send[0] = sums[:TOK].astype(BF16)
            sums_send[1] = sums[2 * TOK :].astype(BF16)
            own_sums = sums[TOK : 2 * TOK]
            sums_copies = [
                send(sums_send.at[(ds + 1) // 2], sums_recv.at[(ds + 1) // 2], ds) for ds in SIDES
            ]

    for n in range(LAYERS - 1, -1, -1):
        d_transit = nn(trans_out_ref[n], gradient.astype(BF16))
        d_wide = jnp.concatenate(
            [(d_transit * back_a[n]).astype(BF16), (d_transit * silu_a[n]).astype(BF16)], axis=0
        )
        d_mid = gradient + norm_back(normal_m[n], scale_m[n], nn(trans_in_ref[n], d_wide))
        d_gated = nn(attn_out_ref[n], d_mid.astype(BF16))
        d_att = by_head(flip(d_gated * gating[n]))
        d_gate = (d_gated * gate_back[n]).astype(BF16)
        dkv_send[n, 1] = nn(soft_b[n, ATOMS:], d_att).astype(BF16)
        wait_for = [
            send(dkv_send.at[n, 1, pl.ds(0, HALF)], dkv_recv.at[n, 1, pl.ds(0, HALF)], 1),
            send(dkv_send.at[n, 1, pl.ds(HALF, HALF)], dkv_recv.at[n, 1, pl.ds(HALF, HALF)], -1),
        ]
        own_d = nt(kv[n, :ATOMS, CA:], d_att)
        halo_d = nt(kv[n, ATOMS:, CA:], d_att)
        own_prod = soft[n, :ATOMS] * own_d
        halo_prod = soft[n, ATOMS:] * halo_d
        inner = jnp.sum(own_prod, axis=0, keepdims=True) + jnp.sum(
            halo_prod, axis=0, keepdims=True
        )
        halo_ds = ((halo_prod - soft[n, ATOMS:] * inner) * SCALE).astype(BF16)
        own_ds = ((own_prod - soft[n, :ATOMS] * inner) * SCALE).astype(BF16)
        dkv_send[n, 0] = nn(halo_ds, q_heads[n]).astype(BF16)
        wait_for += [
            send(dkv_send.at[n, 0, pl.ds(0, HALF)], dkv_recv.at[n, 0, pl.ds(0, HALF)], 1),
            send(dkv_send.at[n, 0, pl.ds(HALF, HALF)], dkv_recv.at[n, 0, pl.ds(HALF, HALF)], -1),
        ]
        d_queries = jnp.concatenate(
            [
                nn(
                    key_t[n, width * h : width * (h + 1), :ATOMS],
                    own_ds[:, ATOMS * h : ATOMS * (h + 1)],
                )
                + nn(
                    key_t[n, width * h : width * (h + 1), ATOMS:],
                    halo_ds[:, ATOMS * h : ATOMS * (h + 1)],
                )
                for h in range(HEADS)
            ],
            axis=0,
        ).astype(BF16)
        own_keys = nn(own_ds, q_heads[n])
        own_vals = nn(soft_b[n, :ATOMS], d_att)
        d_normed = nn(attn_in_ref[n, :, :CA], d_queries) + nn(attn_in_ref[n, :, 3 * CA :], d_gate)
        for copy in wait_for:
            copy.wait_recv()
        d_keys = (own_keys + dkv_recv[n, 0].astype(F32)).astype(BF16)
        d_vals = (own_vals + dkv_recv[n, 1].astype(F32)).astype(BF16)
        d_normed = (
            d_normed
            + nt(attn_in_ref[n, :, CA : 2 * CA], d_keys)
            + nt(attn_in_ref[n, :, 2 * CA : 3 * CA], d_vals)
        )
        gradient = d_mid + norm_back(normal_x[n], scale_x[n], d_normed)

    grad_rows = flip(gradient)
    high, rest = split(grad_rows)
    grad_out[...] = high
    d_cond = nn(pick, high) + nn(pick, rest)
    cond_send[0] = d_cond[:TOK].astype(BF16)
    cond_send[1] = d_cond[2 * TOK :].astype(BF16)
    cond_copies = [send(cond_send.at[(ds + 1) // 2], cond_recv.at[(ds + 1) // 2], ds) for ds in SIDES]
    for copy in sums_copies:
        copy.wait_recv()
    token_sums = own_sums + (sums_recv[0].astype(F32) + sums_recv[1].astype(F32))
    diagonal = iota((TOK, TOK), 0) == iota((TOK, TOK), 1)
    counts = jnp.sum(
        jnp.where(diagonal, counts_ref[...].astype(F32), 0.0), axis=1, keepdims=True
    )
    act_out[...] = (token_sums / counts).astype(BF16)
    for copy in cond_copies:
        copy.wait_recv()
    d_cond = d_cond[TOK : 2 * TOK] + (cond_recv[0].astype(F32) + cond_recv[1].astype(F32))
    high, rest = split(d_cond)
    single_out[...] = (nt(high, proj_ref[...]) + nt(rest, proj_ref[...])).astype(BF16)
    for copy in copies:
        copy.wait_send()


N_COPIES = 5 + 2 + 2 + 11 + 5 + 1 + 2 * (LAYERS - 1) + 2 + 4 * LAYERS + 2


def local(
    atom_single,
    token_single,
    pair_band,
    token_counts,
    atom_token,
    window_starts,
    single_proj,
    pair_proj,
    attn_in,
    attn_out,
    trans_in,
    trans_out,
    agg_proj,
    token_cot,
):
    vmem = pl.BlockSpec(memory_space=pltpu.VMEM)
    smem = pl.BlockSpec(memory_space=pltpu.SMEM)

    def scratch(dtype, *shape):
        return pltpu.VMEM(shape, dtype)

    return pl.pallas_call(
        kernel,
        out_shape=(
            jax.ShapeDtypeStruct((TOK, ACT), BF16),
            jax.ShapeDtypeStruct((ATOMS, CA), BF16),
            jax.ShapeDtypeStruct((TOK, COND), BF16),
        ),
        in_specs=[vmem] * 5 + [smem] + [vmem] * 8,
        out_specs=(vmem, vmem, vmem),
        scratch_shapes=[
            scratch(jnp.int32, 3, 1, ATOMS),
            scratch(BF16, ATOMS, CA),
            scratch(F32, 3, 2, TOK, CA),
            scratch(BF16, 3, 2 * PAIR_PAD, 2 * CA),
            scratch(BF16, 3, 2, TOK, ACT),
            scratch(BF16, CA, ACT),
            scratch(BF16, LAYERS, EXT, 2 * CA),
            scratch(F32, LAYERS, EXT, ALL),
            scratch(BF16, EXT, 6 * CA),
            scratch(BF16, LAYERS, CA, CA),
            scratch(BF16, LAYERS, CA, CA),
            scratch(BF16, LAYERS, 2 * FFA, CA),
            scratch(BF16, LAYERS, CA, FFA),
            scratch(F32, LAYERS, EXT, ALL),
            scratch(BF16, LAYERS, EXT, ALL),
            scratch(BF16, LAYERS, ALL, CA),
            scratch(BF16, LAYERS, CA, EXT),
            scratch(F32, LAYERS, CA, ATOMS),
            scratch(F32, LAYERS, 1, ATOMS),
            scratch(F32, LAYERS, CA, ATOMS),
            scratch(F32, LAYERS, 1, ATOMS),
            scratch(F32, LAYERS, CA, ATOMS),
            scratch(F32, LAYERS, CA, ATOMS),
            scratch(F32, LAYERS, FFA, ATOMS),
            scratch(F32, LAYERS, FFA, ATOMS),
            scratch(BF16, LAYERS, 2, ATOMS, CA),
            scratch(BF16, LAYERS, 2, ATOMS, CA),
            scratch(BF16, 2, TOK, ACT),
            scratch(BF16, 2, TOK, ACT),
            scratch(BF16, 2, TOK, CA),
            scratch(BF16, 2, TOK, CA),
            pltpu.SemaphoreType.DMA((N_COPIES,)),
            pltpu.SemaphoreType.DMA((N_COPIES,)),
        ],
        compiler_params=pltpu.CompilerParams(
            collective_id=0, has_side_effects=True, vmem_limit_bytes=48 * 1024 * 1024
        ),
        cost_estimate=pl.CostEstimate(
            flops=2_000_000_000, bytes_accessed=2_000_000, transcendentals=1_000_000
        ),
        name="atoms",
    )(
        atom_single,
        token_single,
        pair_band,
        token_counts.reshape(1, TOK),
        atom_token.reshape(1, ATOMS),
        window_starts,
        single_proj,
        pair_proj,
        attn_in,
        attn_out,
        trans_in,
        trans_out,
        agg_proj,
        token_cot,
    )


def solution(mesh):
    return jax.shard_map(
        local,
        mesh=mesh,
        in_specs=(
            P("seq", None),
            P("seq", "row"),
            P(("seq", "row"), "col", None),
            P("seq"),
            P("seq"),
            P("seq"),
            P("row", None),
            P(),
            P(),
            P(),
            P(),
            P(),
            P(None, "row"),
            P("seq", "row"),
        ),
        out_specs=(P("seq", "row"), P("seq", None), P("seq", "row")),
        check_vma=False,
    )
```

profile of v0, /device:TPU:1, one launch (start us, length us, event | category | flops | bytes accessed | tf_op | source)
XLA Modules:
  0.0 63.3 jit_solution(14122565408767693979)
XLA Ops:
  0.6 0.0 copy-start.6
  0.6 0.0 copy-start.8
  0.7 0.0 copy-start.9
  0.7 0.0 copy-start.10
  0.7 0.0 copy-start.11
  0.7 0.0 copy-start.12
  0.7 0.8 %copy.17.pair_proj_ref = f32[128,12]{1,0:T(8,128)S(1)} copy(f32[128,12]{0,1:T(8,128)} %param.21) | data formatting | bytes 12288 | tf_op args[7]
  1.5 0.0 copy-done.6
  1.5 0.0 copy-done.8
  1.6 0.0 copy-done.9
  1.6 0.0 copy-done.10
  1.6 0.0 copy-done.11
  1.6 0.0 copy-start
  1.6 1.0 %copy-done = bf16[3,128,512]{2,1,0:T(8,128)(2,1)S(1)} copy-done((bf16[3,128,512]{2,1,0:T(8,128)(2,1)S(1)}, bf16[3,128,512]{2,1,0:T(8,128)(2,1)}, u32[]{:S(2)}) %copy-start) | copy-done | bytes 393240
  2.6 1.0 %copy-done.1 = bf16[3,128,512]{2,1,0:T(8,128)(2,1)S(1)} copy-done((bf16[3,128,512]{2,1,0:T(8,128)(2,1)S(1)}, bf16[3,128,512]{2,1,0:T(8,128)(2,1)}, u32[]{:S(2)}) %copy-start.1) | copy-done | bytes 393240
  3.6 0.9 %copy-done.2 = bf16[3,256,128]{2,1,0:T(8,128)(2,1)S(1)} copy-done((bf16[3,256,128]{2,1,0:T(8,128)(2,1)S(1)}, bf16[3,256,128]{2,1,0:T(8,128)(2,1)}, u32[]{:S(2)}) %copy-start.2) | copy-done | bytes 196632
  4.5 0.9 %copy-done.3 = bf16[3,128,128]{2,1,0:T(8,128)(2,1)S(1)} copy-done((bf16[3,128,128]{2,1,0:T(8,128)(2,1)S(1)}, bf16[3,128,128]{2,1,0:T(8,128)(2,1)}, u32[]{:S(2)}) %copy-start.3) | copy-done | bytes 98328
  5.4 0.9 %copy-done.4 = bf16[128,384]{1,0:T(8,128)(2,1)S(1)} copy-done((bf16[128,384]{1,0:T(8,128)(2,1)S(1)}, bf16[128,384]{1,0:T(8,128)(2,1)}, u32[]{:S(2)}) %copy-start.4) | copy-done | bytes 98328
  6.3 0.9 %copy-done.5 = bf16[8,40,128]{2,1,0:T(8,128)(2,1)S(1)} copy-done((bf16[8,40,128]{2,1,0:T(8,128)(2,1)S(1)}, bf16[8,40,128]{2,1,0:T(8,128)(2,1)}, u32[]{:S(2)}) %copy-start.5) | copy-done | bytes 81944
  7.2 0.8 %copy-done.7 = bf16[128,128]{1,0:T(8,128)(2,1)S(1)} copy-done((bf16[128,128]{1,0:T(8,128)(2,1)S(1)}, bf16[128,128]{1,0:T(8,128)(2,1)}, u32[]{:S(2)}) %copy-start.7) | copy-done | bytes 32792
  7.9 53.6 %atoms.1 = (bf16[16,384]{1,0:T(8,128)(2,1)S(1)}, bf16[128,128]{1,0:T(8,128)(2,1)S(1)}, bf16[16,192]{1,0:T(8,128)(2,1)S(1)}) custom-call(bf16[128,128]{1,0:T(8,128)(2,1)S(1)} %copy-done.7, bf16[16,192]{1,0:T(8,128)(2,1)S(1)} %copy-done.9, bf16[8,40,128]{2,1,0:T(8,128)(2,1)S(1)} %copy-done.5, s32[1,16]{1,0:T(1,128)S(1)} %bitcast.2, s32[1,128]{1,0:T(1,128)S(1)} %bitcast.3, ...), custom_call_target="tpu_custom_call" | custom-call | flops 2000000000 | bytes 2000000 | tf_op jit(solution)/shard_map/atoms/pallas_call | solution.py:491
  61.5 0.6 copy.21
  62.1 0.6 copy.22
  62.7 0.6 copy.23
  (7 shorter events, 0.0 us)
Async XLA Ops:
  0.6 0.9 %copy-start.6 = (bf16[192,128]{1,0:T(8,128)(2,1)S(1)}, bf16[192,128]{1,0:T(8,128)(2,1)}, u32[]{:S(2)}) copy-start(bf16[192,128]{1,0:T(8,128)(2,1)} %proj_ref.1) | copy-start | bytes 147460
  0.6 0.9 %copy-start.8 = (bf16[16,384]{1,0:T(8,128)(2,1)S(1)}, bf16[16,384]{1,0:T(8,128)(2,1)}, u32[]{:S(2)}) copy-start(bf16[16,384]{1,0:T(8,128)(2,1)} %cot_ref.1) | copy-start | bytes 36868
  0.7 0.9 %copy-start.9 = (bf16[16,192]{1,0:T(8,128)(2,1)S(1)}, bf16[16,192]{1,0:T(8,128)(2,1)}, u32[]{:S(2)}) copy-start(bf16[16,192]{1,0:T(8,128)(2,1)} %single_ref.1) | copy-start | bytes 18436
  0.7 0.9 %copy-start.10 = (s32[16]{0:T(128)S(1)}, s32[16]{0:T(128)}, u32[]{:S(2)}) copy-start(s32[16]{0:T(128)} %param.17) | copy-start | bytes 196
  0.7 0.9 %copy-start.11 = (s32[128]{0:T(128)S(1)}, s32[128]{0:T(128)}, u32[]{:S(2)}) copy-start(s32[128]{0:T(128)} %param.18) | copy-start | bytes 1540
  0.7 0.9 %copy-start.12 = (s32[4]{0:T(128)S(1)}, s32[4]{0:T(128)}, u32[]{:S(2)}) copy-start(s32[4]{0:T(128)} %starts_ref.1) | copy-start | bytes 52
  1.6 1.0 %copy-start = (bf16[3,128,512]{2,1,0:T(8,128)(2,1)S(1)}, bf16[3,128,512]{2,1,0:T(8,128)(2,1)}, u32[]{:S(2)}) copy-start(bf16[3,128,512]{2,1,0:T(8,128)(2,1)} %attn_in_ref.1) | copy-start | bytes 1179652
  2.6 1.0 %copy-start.1 = (bf16[3,128,512]{2,1,0:T(8,128)(2,1)S(1)}, bf16[3,128,512]{2,1,0:T(8,128)(2,1)}, u32[]{:S(2)}) copy-start(bf16[3,128,512]{2,1,0:T(8,128)(2,1)} %trans_in_ref.1) | copy-start | bytes 1179652
  3.6 0.9 %copy-start.2 = (bf16[3,256,128]{2,1,0:T(8,128)(2,1)S(1)}, bf16[3,256,128]{2,1,0:T(8,128)(2,1)}, u32[]{:S(2)}) copy-start(bf16[3,256,128]{2,1,0:T(8,128)(2,1)} %trans_out_ref.1) | copy-start | bytes 589828
  4.5 0.9 %copy-start.3 = (bf16[3,128,128]{2,1,0:T(8,128)(2,1)S(1)}, bf16[3,128,128]{2,1,0:T(8,128)(2,1)}, u32[]{:S(2)}) copy-start(bf16[3,128,128]{2,1,0:T(8,128)(2,1)} %attn_out_ref.1) | copy-start | bytes 294916
  5.4 0.9 %copy-start.4 = (bf16[128,384]{1,0:T(8,128)(2,1)S(1)}, bf16[128,384]{1,0:T(8,128)(2,1)}, u32[]{:S(2)}) copy-start(bf16[128,384]{1,0:T(8,128)(2,1)} %agg_ref.1) | copy-start | bytes 294916
  6.3 0.9 %copy-start.5 = (bf16[8,40,128]{2,1,0:T(8,128)(2,1)S(1)}, bf16[8,40,128]{2,1,0:T(8,128)(2,1)}, u32[]{:S(2)}) copy-start(bf16[8,40,128]{2,1,0:T(8,128)(2,1)} %band_ref.1) | copy-start | bytes 245764
  7.2 0.8 %copy-start.7 = (bf16[128,128]{1,0:T(8,128)(2,1)S(1)}, bf16[128,128]{1,0:T(8,128)(2,1)}, u32[]{:S(2)}) copy-start(bf16[128,128]{1,0:T(8,128)(2,1)} %atom_ref.1) | copy-start | bytes 98308
where the time goes:
time: 63.8 us; the launch traced here: 63.3 us
  Pallas kernels  53.6 us (84%)
  local copies, waits for them, and re-layouts  9.02 us (14%)
  between operations  0.75 us (1%)
    pallas_call x1, Pallas kernels, local(): pl.pallas_call(kernel, out_shape=(jax.ShapeDtypeStruct((TOK, ACT), BF16),...  53.6 us
    unnamed x30, local copies, waits for them, and re-layouts  9.02 us

commit v1 on v0

v1 whole, which is shorter than its diff:
```python
import functools

import jax
import jax.numpy as jnp
from jax import lax
from jax.experimental import pallas as pl
from jax.experimental.pallas import tpu as pltpu
from jax.sharding import PartitionSpec as P

HEADS = 4
QB = 32
KW = 128
LAYERS = 3
ATOMS = 128
CA = 128
TOK = 16
COND = 192
ACT = 384
FFA = 256
PAIR_ROWS = 8
PAIR_COLS = 40
PAIR_PAD = 48
SPAN = 3 * TOK
HALF = 64
EXT = 256
ALL = HEADS * ATOMS
F32 = jnp.float32
BF16 = jnp.bfloat16
EPS = 1e-05
SCALE = (CA // HEADS) ** (-0.5)
MESH = pl.DeviceIdType.MESH

PARTNERS = [
    (ds, dr, dc)
    for ds in (0, -1, 1)
    for dr in (0, 1)
    for dc in (0, 1)
    if (ds, dr, dc) != (0, 0, 0)
]
COND_PARTNERS = [p for p in PARTNERS if p[2] == 0]
SIDES = (-1, 1)


def nn(a, b):
    return lax.dot_general(a, b, (((1,), (0,)), ((), ())), preferred_element_type=F32)


def nt(a, b):
    return lax.dot_general(a, b, (((1,), (1,)), ((), ())), preferred_element_type=F32)


def tn(a, b):
    return lax.dot_general(a, b, (((0,), (0,)), ((), ())), preferred_element_type=F32)


def flip(values):
    return jnp.transpose(values, (1, 0))


def iota(shape, dim):
    return lax.broadcasted_iota(jnp.int32, shape, dim)


def norm_rows(values):
    centre = values - jnp.mean(values, axis=0, keepdims=True)
    scaling = lax.rsqrt(jnp.mean(centre * centre, axis=0, keepdims=True) + EPS)
    return centre * scaling, scaling


def norm_back(normal, scaling, upstream):
    return scaling * (
        upstream
        - jnp.mean(upstream, axis=0, keepdims=True)
        - normal * jnp.mean(upstream * normal, axis=0, keepdims=True)
    )


def by_head(rows):
    head = iota(rows.shape, 1) // (CA // HEADS)
    return jnp.concatenate(
        [jnp.where(head == h, rows, 0.0).astype(BF16) for h in range(HEADS)], axis=0
    )


def split(values):
    high = values.astype(BF16)
    return high, (values - high.astype(F32)).astype(BF16)


def kernel(
    atom_hbm,
    single_hbm,
    band_hbm,
    counts_hbm,
    ids_hbm,
    starts_hbm,
    proj_hbm,
    pair_proj_hbm,
    attn_in_hbm,
    attn_out_hbm,
    trans_in_hbm,
    trans_out_hbm,
    agg_hbm,
    cot_hbm,
    act_out,
    grad_out,
    single_out,
    atom_ref,
    single_ref,
    band_ref,
    counts_ref,
    ids_ref,
    starts_ref,
    proj_ref,
    pair_proj_ref,
    attn_in_ref,
    attn_out_ref,
    trans_in_ref,
    trans_out_ref,
    agg_ref,
    id_buf,
    halo_buf,
    cond_buf,
    pair_buf,
    cot_buf,
    agg_buf,
    rows_buf,
    stream_buf,
    kv,
    kv_wide,
    bias,
    bias_rim,
    mixed,
    gate_t,
    out_t,
    in_t,
    down_t,
    soft,
    soft_b,
    soft_rim,
    soft_rim_own,
    q_heads,
    q_rim,
    key_t,
    normal_x,
    scale_x,
    normal_m,
    scale_m,
    gating,
    gate_back,
    silu_a,
    back_a,
    dkv_send,
    dkv_recv,
    part_send,
    part_recv,
    sums_send,
    sums_recv,
    cond_send,
    cond_recv,
    local_sem,
    send_sem,
    recv_sem,
):
    seq = lax.axis_index("seq")
    row = lax.axis_index("row")
    col = lax.axis_index("col")
    seqs = lax.axis_size("seq")
    width = CA // HEADS

    def partner(ds, dr, dc):
        return (
            lax.rem(seq + ds + seqs, seqs),
            lax.rem(row + dr, 2),
            lax.rem(col + dc, 2),
        )

    copies = []

    def send(src, dst, ds, dr=0, dc=0):
        place = len(copies)
        copy = pltpu.make_async_remote_copy(
            src_ref=src,
            dst_ref=dst,
            send_sem=send_sem.at[place],
            recv_sem=recv_sem.at[place],
            device_id=partner(ds, dr, dc),
            device_id_type=MESH,
        )
        copy.start()
        copies.append(copy)
        return copy

    def arrive(group):
        for copy in group:
            copy.wait_recv()

    barrier = pltpu.get_barrier_semaphore()
    for ds, dr, dc in PARTNERS:
        pl.semaphore_signal(barrier, inc=1, device_id=partner(ds, dr, dc), device_id_type=MESH)

    fetches = []

    def fetch(src, dst):
        copy = pltpu.make_async_copy(src, dst, local_sem.at[len(fetches)])
        copy.start()
        fetches.append(copy)
        return copy

    first_fetch = [fetch(single_hbm, single_ref), fetch(proj_hbm, proj_ref)]
    pair_fetch = [fetch(band_hbm, band_ref), fetch(pair_proj_hbm, pair_proj_ref)]
    id_fetch = [fetch(ids_hbm, ids_ref), fetch(starts_hbm, starts_ref)]
    atom_fetch = [fetch(atom_hbm, atom_ref)]
    weight_fetch = [
        fetch(attn_in_hbm, attn_in_ref),
        fetch(attn_out_hbm, attn_out_ref),
        fetch(trans_in_hbm, trans_in_ref),
        fetch(trans_out_hbm, trans_out_ref),
        fetch(agg_hbm, agg_ref),
        fetch(cot_hbm, cot_buf.at[1, 0]),
        fetch(counts_hbm, counts_ref),
    ]

    for copy in first_fetch:
        copy.wait()
    cond_buf[1, 0] = nn(single_ref[...], proj_ref[...])
    for copy in id_fetch:
        copy.wait()
    lane = iota((1, ATOMS), 1)
    own_first = jnp.zeros((1, ATOMS), jnp.int32)
    for b in range(ATOMS // QB):
        own_first = jnp.where(lane // QB == b, starts_ref[b], own_first)
    id_buf[1, 0:1] = ids_ref[...]
    id_buf[1, 1:2] = own_first
    for copy in pair_fetch:
        copy.wait()
    place_h = (iota((LAYERS * HEADS, CA), 1) == 8 * iota((LAYERS * HEADS, CA), 0)).astype(BF16)
    pp_high, pp_rest = split(pair_proj_ref[...])
    spread_high = tn(pp_high, place_h).astype(BF16)
    spread_rest = tn(pp_rest, place_h).astype(BF16)
    band = band_ref[...].astype(F32).reshape(PAIR_ROWS * PAIR_COLS, CA)
    centre = band - jnp.mean(band, axis=1, keepdims=True)
    normal = centre * lax.rsqrt(jnp.mean(centre * centre, axis=1, keepdims=True) + EPS)
    n_high, n_rest = split(normal)
    pairs = nn(n_high, spread_high) + nn(n_high, spread_rest) + nn(n_rest, spread_high)
    tile = pairs[:PAIR_COLS]
    for i in range(1, PAIR_ROWS):
        tile = tile + pltpu.roll(pairs[PAIR_COLS * i : PAIR_COLS * (i + 1)], i, 1)
    tile = jnp.concatenate([tile, jnp.zeros((PAIR_PAD - PAIR_COLS, CA), F32)], axis=0)
    pair_rows = pl.ds(pl.multiple_of(col * PAIR_PAD, 16), PAIR_PAD)
    pair_lanes = pl.ds(pl.multiple_of(row * CA, CA), CA)
    pair_buf[1, pair_rows, pair_lanes] = tile.astype(BF16)

    pl.semaphore_wait(barrier, len(PARTNERS))

    cond_copies = [
        send(cond_buf.at[1, 0], cond_buf.at[1 - ds, dr], ds, dr) for ds, dr, dc in COND_PARTNERS
    ]
    id_copies = [send(id_buf.at[1], id_buf.at[1 - ds], ds) for ds in SIDES]
    halo_copies = [
        send(atom_hbm.at[pl.ds(0, HALF)], halo_buf.at[pl.ds(0, HALF)], -1),
        send(atom_hbm.at[pl.ds(HALF, HALF)], halo_buf.at[pl.ds(HALF, HALF)], 1),
    ]
    pair_copies = [
        send(
            pair_buf.at[1, pair_rows, pair_lanes],
            pair_buf.at[1 - ds, pair_rows, pair_lanes],
            ds,
            dr,
            dc,
        )
        for ds, dr, dc in PARTNERS
    ]
    cot_copies = [
        send(cot_hbm, cot_buf.at[1 - ds, dr], ds, dr) for ds, dr, dc in COND_PARTNERS
    ]
    agg_copy = send(agg_hbm, agg_buf, 0, 1)

    for copy in atom_fetch + weight_fetch:
        copy.wait()
    for n in range(LAYERS):
        gate_t[n] = flip(attn_in_ref[n, :, 3 * CA :])
        out_t[n] = flip(attn_out_ref[n])
        in_t[n] = flip(trans_in_ref[n])
        down_t[n] = flip(trans_out_ref[n])

    token_base = TOK * (seq - 1)
    atom_base = seq * ATOMS
    low = lane < HALF

    def as_cols(ids):
        return flip(jnp.broadcast_to(ids.astype(F32), (CA, ATOMS))).astype(jnp.int32)

    own_ids = ids_ref[...] - token_base
    own_id_cols = as_cols(own_ids)
    atom_t = flip(atom_ref[...].astype(F32))

    arrive(id_copies + halo_copies + cond_copies)
    left_ids = id_buf[0, 0:1] - token_base
    right_ids = id_buf[2, 0:1] - token_base
    halo_ids = jnp.where(low, right_ids, left_ids)
    halo_id_cols = as_cols(halo_ids)
    pick_ext = (iota((SPAN, EXT), 0) == jnp.concatenate([own_ids, halo_ids], axis=1)).astype(
        F32
    ).astype(BF16)
    pick = pick_ext[:, :ATOMS]
    cond = (cond_buf[:, 0] + cond_buf[:, 1]).astype(BF16).reshape(SPAN, CA)
    cond_t = flip(cond.astype(F32)).astype(BF16)
    stream_ext = jnp.concatenate([atom_t, flip(halo_buf[...].astype(F32))], axis=1) + nn(
        cond_t, pick_ext
    )

    position = iota((EXT, ATOMS), 0)
    position = jnp.where(position < ATOMS + HALF, position, position - EXT)
    first = own_first - atom_base
    outside = jnp.where((position >= first) & (position < first + KW), 0.0, -1e30)
    outside = jnp.concatenate([outside] * HEADS, axis=1)

    wide = 3 * 2 * CA
    place = iota((wide, ATOMS), 0)
    head_of = (place // PAIR_ROWS) % (CA // PAIR_ROWS)
    token_of = TOK * (place // (2 * CA)) + PAIR_ROWS * ((place // CA) % 2) + place % PAIR_ROWS

    def mix_bias(at, id_cols):
        rows = id_cols.shape[0]
        lanes = iota((rows, 2 * PAIR_PAD), 1)
        column = jnp.where(
            lanes < PAIR_PAD,
            jnp.where(lanes < PAIR_COLS, lanes, -4096),
            jnp.where(lanes < PAIR_PAD + PAIR_COLS, lanes - (PAIR_PAD - PAIR_COLS), -4096),
        )
        for s in range(3):
            take = (id_cols[:, : 2 * PAIR_PAD] + (2 - s) * TOK == column).astype(F32).astype(BF16)
            mixed[at : at + rows, 2 * CA * s : 2 * CA * (s + 1)] = nn(take, pair_buf[s]).astype(
                BF16
            )

    def bias_picks(n, ids):
        hit = token_of == ids
        return jnp.concatenate(
            [
                (hit & (head_of == HEADS * n + h)).astype(F32).astype(BF16)
                for h in range(HEADS)
            ],
            axis=1,
        )

    def bias_layer(n):
        bias[n] = nn(mixed[:EXT], bias_picks(n, own_ids)) + outside

    def right_rows(values):
        return jnp.concatenate(
            [values[HALF:ATOMS], values[ATOMS : ATOMS + HALF], values[EXT : EXT + HALF]], axis=0
        )

    def left_rows(values):
        return jnp.concatenate(
            [values[:HALF], values[ATOMS + HALF : EXT], values[EXT + HALF :]], axis=0
        )

    low_all = jnp.concatenate([low] * HEADS, axis=1)

    def attend_own(n, kv_n, wait_for):
        own_scores = nt(kv_n[:ATOMS, :CA], q_heads[n]) * SCALE + bias[n, :ATOMS]
        own_values = flip(kv_n[:ATOMS, CA:])
        arrive(wait_for)
        halo_scores = nt(kv_n[ATOMS:EXT, :CA], q_heads[n]) * SCALE + bias[n, ATOMS:]
        halo_values = flip(kv_n[ATOMS:EXT, CA:])
        most = jnp.maximum(
            jnp.max(own_scores, axis=0, keepdims=True), jnp.max(halo_scores, axis=0, keepdims=True)
        )
        own_exp = jnp.exp(own_scores - most)
        halo_exp = jnp.exp(halo_scores - most)
        total = jnp.sum(own_exp, axis=0, keepdims=True) + jnp.sum(halo_exp, axis=0, keepdims=True)
        share = 1.0 / total
        own_soft = own_exp * share
        halo_soft = halo_exp * share
        soft[n, :ATOMS] = own_soft
        soft[n, ATOMS:] = halo_soft
        soft_b[n, :ATOMS] = own_soft.astype(BF16)
        soft_b[n, ATOMS:] = halo_soft.astype(BF16)
        values_t = jnp.concatenate([own_values, halo_values], axis=1)
        key_t[n, :, :ATOMS] = flip(kv_n[:ATOMS, :CA])
        key_t[n, :, ATOMS:] = flip(kv_n[ATOMS:EXT, :CA])
        return jnp.concatenate(
            [
                nn(
                    values_t[width * h : width * (h + 1)],
                    soft_b[n, :, ATOMS * h : ATOMS * (h + 1)],
                )
                for h in range(HEADS)
            ],
            axis=0,
        )

    def attend_rim(n, kv_n):
        right_kv = right_rows(kv_n)
        left_kv = left_rows(kv_n)
        scores = jnp.where(
            low_all, nt(right_kv[:, :CA], q_rim[...]), nt(left_kv[:, :CA], q_rim[...])
        )
        scores = scores * SCALE + bias_rim[...]
        most = jnp.maximum(jnp.max(scores, axis=0, keepdims=True), -1e29)
        exps = jnp.exp(scores - most)
        weights = exps * (1.0 / jnp.maximum(jnp.sum(exps, axis=0, keepdims=True), 1e-30))
        soft_rim[...] = weights
        rounded = weights.astype(BF16)
        near = weights[:HALF]
        soft_rim_own[:HALF] = jnp.where(low_all, 0.0, near).astype(BF16)
        soft_rim_own[HALF:] = jnp.where(low_all, near, 0.0).astype(BF16)
        right_t = flip(right_kv[:, CA:])
        left_t = flip(left_kv[:, CA:])
        parts = []
        for h in range(HEADS):
            here = rounded[:, ATOMS * h : ATOMS * (h + 1)]
            parts.append(
                jnp.where(
                    low,
                    nn(right_t[width * h : width * (h + 1)], here),
                    nn(left_t[width * h : width * (h + 1)], here),
                )
            )
        return jnp.concatenate(parts, axis=0)

    def transition(n, stream, gates, attended, lanes):
        gated = gates * attended
        gating[n, :, :lanes] = gates
        gate_back[n] = gated[:, :ATOMS] * (1.0 - gates[:, :ATOMS])
        x_mid = stream + nn(out_t[n], gated.astype(BF16))
        normal, scaling = norm_rows(x_mid)
        normal_m[n, :, :lanes] = normal
        scale_m[n, :, :lanes] = scaling
        widened = nn(in_t[n], normal.astype(BF16))
        part_a = widened[:FFA]
        part_b = widened[FFA:]
        sig = jax.nn.sigmoid(part_a)
        act = part_a * sig
        silu_a[n, :, :lanes] = act
        back_a[n, :, :lanes] = part_b * (sig * (1.0 + part_a * (1.0 - sig)))
        return x_mid + nn(down_t[n], (act * part_b).astype(BF16))

    def local_layer(n, stream_ext):
        normal_ext, scale_ext = norm_rows(stream_ext)
        normal_x[n] = normal_ext
        scale_x[n] = scale_ext
        rows_ext = flip(normal_ext).astype(BF16)
        kv[n // 2] = nn(rows_ext, attn_in_ref[n, :, CA : 3 * CA]).astype(BF16)
        queries = nn(rows_ext[:ATOMS], attn_in_ref[n, :, :CA]).astype(BF16).astype(F32)
        q_heads[n] = by_head(queries)
        gates = jax.nn.sigmoid(nn(gate_t[n], normal_ext[:, :ATOMS].astype(BF16)))
        if n == 0:
            arrive(pair_copies)
            mix_bias(0, jnp.concatenate([own_id_cols, halo_id_cols], axis=0))
            bias_layer(n)
        attended = attend_own(n, kv[n // 2], [])
        return transition(n, stream_ext[:, :ATOMS], gates, attended, ATOMS)

    stream = local_layer(0, stream_ext)

    normal, scaling = norm_rows(stream)
    normal_x[1, :, :ATOMS] = normal
    scale_x[1, :, :ATOMS] = scaling
    rows_buf[:ATOMS] = flip(normal).astype(BF16)
    lower, upper = pl.ds(0, HALF), pl.ds(HALF, HALF)
    inner_copies = [
        send(rows_buf.at[lower], rows_buf.at[pl.ds(ATOMS, HALF)], -1),
        send(rows_buf.at[upper], rows_buf.at[pl.ds(ATOMS + HALF, HALF)], 1),
    ]
    outer_copies = [
        send(rows_buf.at[upper], rows_buf.at[pl.ds(EXT, HALF)], -1),
        send(rows_buf.at[lower], rows_buf.at[pl.ds(EXT + HALF, HALF)], 1),
    ]
    stream_buf[0] = flip(stream)
    stream_copies = [
        send(stream_buf.at[0, lower], stream_buf.at[1, lower], -1),
        send(stream_buf.at[0, upper], stream_buf.at[1, upper], 1),
    ]
    kv_wide[:ATOMS] = nn(rows_buf[:ATOMS], attn_in_ref[1, :, CA : 3 * CA]).astype(BF16)
    q_heads[1] = by_head(nn(rows_buf[:ATOMS], attn_in_ref[1, :, :CA]).astype(BF16).astype(F32))
    bias_layer(1)
    outer_ids = pltpu.roll(jnp.where(low, left_ids, right_ids), HALF, 1)
    mix_bias(EXT, as_cols(outer_ids))
    rim_full = nn(mixed[...], bias_picks(1, halo_ids))
    rim_rows = iota((3 * HALF, ATOMS), 0)
    left_position = jnp.where(
        rim_rows < HALF,
        rim_rows,
        jnp.where(rim_rows < ATOMS, rim_rows - ATOMS, rim_rows - EXT),
    )
    rim_position = jnp.where(low, HALF + rim_rows, left_position)
    rim_first = jnp.where(low, id_buf[2, 1:2], id_buf[0, 1:2]) - atom_base
    rim_outside = jnp.where(
        (rim_position >= rim_first) & (rim_position < rim_first + KW), 0.0, -1e30
    )
    bias_rim[...] = jnp.where(low_all, right_rows(rim_full), left_rows(rim_full)) + jnp.concatenate(
        [rim_outside] * HEADS, axis=1
    )
    bias_layer(2)
    at_token = jnp.concatenate([own_id_cols, halo_id_cols], axis=0) == iota((EXT, CA), 1)
    pick_t = at_token[:ATOMS].astype(F32).astype(BF16)[:, :SPAN]
    token_atoms = jnp.sum(at_token.astype(F32), axis=0, keepdims=True)
    atom_counts = jnp.sum(jnp.where(at_token[:ATOMS], token_atoms, 0.0), axis=1, keepdims=True)
    inverse = 1.0 / jnp.maximum(atom_counts, 1.0)
    arrive(inner_copies)
    kv_wide[ATOMS:EXT] = nn(rows_buf[ATOMS:EXT], attn_in_ref[1, :, CA : 3 * CA]).astype(BF16)
    attended = attend_own(1, kv_wide, [])
    gates = jax.nn.sigmoid(nt(gate_t[1], rows_buf[:EXT]))
    q_rim[...] = by_head(nn(rows_buf[ATOMS:EXT], attn_in_ref[1, :, :CA]).astype(BF16).astype(F32))
    arrive(outer_copies)
    kv_wide[EXT:] = nn(rows_buf[EXT:], attn_in_ref[1, :, CA : 3 * CA]).astype(BF16)
    attended = jnp.concatenate([attended, attend_rim(1, kv_wide)], axis=1)
    arrive(stream_copies)
    stream_ext = jnp.concatenate([stream, flip(stream_buf[1])], axis=1)
    stream_ext = transition(1, stream_ext, gates, attended, EXT)

    stream = local_layer(2, stream_ext)

    final = flip(stream).astype(BF16)
    arrive([agg_copy] + cot_copies)
    gradient = None
    for part in range(2):
        weights = agg_ref[...] if part == 0 else agg_buf[...]
        pre = nn(final, weights)
        sig = jax.nn.sigmoid(pre)
        d_act = nn(pick_t, cot_buf[:, part].reshape(SPAN, ACT)) * inverse
        d_pre = (d_act * (sig * (1.0 + pre * (1.0 - sig)))).astype(BF16)
        term = nt(weights, d_pre)
        gradient = term if part == 0 else gradient + term
        if part == 0:
            high, rest = split(pre * sig)
            sums = nn(pick, high) + nn(pick, rest)
            sums_send[0] = sums[:TOK].astype(BF16)
            sums_send[1] = sums[2 * TOK :].astype(BF16)
            own_sums = sums[TOK : 2 * TOK]
            sums_copies = [
                send(sums_send.at[(ds + 1) // 2], sums_recv.at[(ds + 1) // 2], ds) for ds in SIDES
            ]

    def d_middle(n, upstream, lanes):
        d_transit = nn(trans_out_ref[n], upstream.astype(BF16))
        d_wide = jnp.concatenate(
            [
                (d_transit * back_a[n, :, :lanes]).astype(BF16),
                (d_transit * silu_a[n, :, :lanes]).astype(BF16),
            ],
            axis=0,
        )
        d_mid = upstream + norm_back(
            normal_m[n, :, :lanes], scale_m[n, :, :lanes], nn(trans_in_ref[n], d_wide)
        )
        return d_mid, nn(attn_out_ref[n], d_mid.astype(BF16))

    def d_own(n, kv_n, d_att, sent):
        own_d = nt(kv_n[:ATOMS, CA:], d_att)
        halo_d = nt(kv_n[ATOMS:EXT, CA:], d_att)
        own_prod = soft[n, :ATOMS] * own_d
        halo_prod = soft[n, ATOMS:] * halo_d
        inner = jnp.sum(own_prod, axis=0, keepdims=True) + jnp.sum(
            halo_prod, axis=0, keepdims=True
        )
        halo_ds = ((halo_prod - soft[n, ATOMS:] * inner) * SCALE).astype(BF16)
        own_ds = ((own_prod - soft[n, :ATOMS] * inner) * SCALE).astype(BF16)
        if sent is not None:
            sent(halo_ds)
        d_queries = jnp.concatenate(
            [
                nn(
                    key_t[n, width * h : width * (h + 1), :ATOMS],
                    own_ds[:, ATOMS * h : ATOMS * (h + 1)],
                )
                + nn(
                    key_t[n, width * h : width * (h + 1), ATOMS:],
                    halo_ds[:, ATOMS * h : ATOMS * (h + 1)],
                )
                for h in range(HEADS)
            ],
            axis=0,
        ).astype(BF16)
        return d_queries, nn(own_ds, q_heads[n]), nn(soft_b[n, :ATOMS], d_att)

    def weigh_kv(n, d_keys, d_vals):
        return nt(attn_in_ref[n, :, CA : 2 * CA], d_keys) + nt(
            attn_in_ref[n, :, 2 * CA : 3 * CA], d_vals
        )

    def local_back(n, upstream):
        slot = n // 2
        d_mid, d_gated = d_middle(n, upstream, ATOMS)
        d_att = by_head(flip(d_gated * gating[n, :, :ATOMS]))
        d_gate = (d_gated * gate_back[n]).astype(BF16)
        group = []

        def give(kind, values):
            dkv_send[slot, kind] = values.astype(BF16)
            group.append(
                send(dkv_send.at[slot, kind, lower], dkv_recv.at[slot, kind, lower], 1)
            )
            group.append(
                send(dkv_send.at[slot, kind, upper], dkv_recv.at[slot, kind, upper], -1)
            )

        give(1, nn(soft_b[n, ATOMS:], d_att))
        d_queries, d_keys, d_vals = d_own(
            n, kv[slot], d_att, lambda halo_ds: give(0, nn(halo_ds, q_heads[n]))
        )
        d_normed = (
            nn(attn_in_ref[n, :, :CA], d_queries)
            + nn(attn_in_ref[n, :, 3 * CA :], d_gate)
            + weigh_kv(n, d_keys.astype(BF16), d_vals.astype(BF16))
        )
        part = d_mid + norm_back(normal_x[n, :, :ATOMS], scale_x[n, :, :ATOMS], d_normed)
        return part, group

    def beside(n):
        slot = n // 2
        return norm_back(
            normal_x[n, :, ATOMS:],
            scale_x[n, :, ATOMS:],
            weigh_kv(n, dkv_send[slot, 0], dkv_send[slot, 1]),
        )

    def from_beside(n):
        slot = n // 2
        return norm_back(
            normal_x[n, :, :ATOMS],
            scale_x[n, :, :ATOMS],
            weigh_kv(n, dkv_recv[slot, 0], dkv_recv[slot, 1]),
        )

    part, group = local_back(2, gradient)
    part_send[...] = part.astype(BF16)
    part_copies = [send(part_send, part_recv.at[(ds + 1) // 2], ds) for ds in SIDES]
    halo_gradient = beside(2)
    arrive(group)
    gradient = part + from_beside(2)
    arrive(part_copies)
    halo_gradient = halo_gradient + jnp.where(low, part_recv[0], part_recv[1]).astype(F32)
    gradient = jnp.concatenate([gradient, halo_gradient], axis=1)

    d_mid, d_gated = d_middle(1, gradient, EXT)
    d_att_t = d_gated * gating[1]
    d_att = by_head(flip(d_att_t[:, :ATOMS]))
    d_att_rim = by_head(flip(d_att_t[:, ATOMS:]))
    d_gate = (d_gated[:, :ATOMS] * gate_back[1]).astype(BF16)
    d_queries, d_keys, d_vals = d_own(1, kv_wide, d_att, None)
    rim_d = jnp.where(
        low_all,
        nt(right_rows(kv_wide[:, CA:]), d_att_rim),
        nt(left_rows(kv_wide[:, CA:]), d_att_rim),
    )
    rim_prod = soft_rim[...] * rim_d
    rim_inner = jnp.sum(rim_prod, axis=0, keepdims=True)
    rim_ds = (rim_prod[:HALF] - soft_rim[:HALF] * rim_inner) * SCALE
    rim_ds = jnp.concatenate(
        [jnp.where(low_all, 0.0, rim_ds), jnp.where(low_all, rim_ds, 0.0)], axis=0
    ).astype(BF16)
    d_keys = d_keys + nn(rim_ds, q_rim[...])
    d_vals = d_vals + nn(soft_rim_own[...], d_att_rim)
    d_normed = (
        nn(attn_in_ref[1, :, :CA], d_queries)
        + nn(attn_in_ref[1, :, 3 * CA :], d_gate)
        + weigh_kv(1, d_keys.astype(BF16), d_vals.astype(BF16))
    )
    gradient = d_mid[:, :ATOMS] + norm_back(
        normal_x[1, :, :ATOMS], scale_x[1, :, :ATOMS], d_normed
    )

    def per_token(picks, values):
        high, rest = split(values)
        return nt(picks, high) + nt(picks, rest)

    part, group = local_back(0, gradient)
    d_cond = per_token(pick, part)
    cond_send[0] = d_cond[:TOK].astype(BF16)
    cond_send[1] = d_cond[2 * TOK :].astype(BF16)
    last_copies = [send(cond_send.at[(ds + 1) // 2], cond_recv.at[(ds + 1) // 2], ds) for ds in SIDES]
    d_cond = d_cond[TOK : 2 * TOK] + per_token(pick_ext[TOK : 2 * TOK, ATOMS:], beside(0))
    arrive(sums_copies)
    token_sums = own_sums + (sums_recv[0].astype(F32) + sums_recv[1].astype(F32))
    diagonal = iota((TOK, TOK), 0) == iota((TOK, TOK), 1)
    counts = jnp.sum(
        jnp.where(diagonal, counts_ref[...].astype(F32), 0.0), axis=1, keepdims=True
    )
    act_out[...] = (token_sums / counts).astype(BF16)
    arrive(group)
    rest_gradient = from_beside(0)
    grad_out[...] = flip(part + rest_gradient).astype(BF16)
    d_cond = d_cond + per_token(pick[TOK : 2 * TOK], rest_gradient)
    arrive(last_copies)
    d_cond = d_cond + (cond_recv[0].astype(F32) + cond_recv[1].astype(F32))
    high, rest = split(d_cond)
    single_out[...] = (nt(high, proj_ref[...]) + nt(rest, proj_ref[...])).astype(BF16)
    for copy in copies:
        copy.wait_send()


N_COPIES = 5 + 2 + 2 + 11 + 5 + 1 + 6 + 2 + 4 + 2 + 4 + 2


def hand_on(act, grad, single, act_out, grad_out, single_out):
    act_out[...] = act[...]
    grad_out[...] = grad[...]
    single_out[...] = single[...]


def local(
    atom_single,
    token_single,
    pair_band,
    token_counts,
    atom_token,
    window_starts,
    single_proj,
    pair_proj,
    attn_in,
    attn_out,
    trans_in,
    trans_out,
    agg_proj,
    token_cot,
):
    vmem = pl.BlockSpec(memory_space=pltpu.VMEM)
    hbm = pl.BlockSpec(memory_space=pltpu.HBM)

    def scratch(dtype, *shape):
        return pltpu.VMEM(shape, dtype)

    results = (
        jax.ShapeDtypeStruct((TOK, ACT), BF16),
        jax.ShapeDtypeStruct((ATOMS, CA), BF16),
        jax.ShapeDtypeStruct((TOK, COND), BF16),
    )
    results_here = pl.pallas_call(
        kernel,
        out_shape=results,
        in_specs=[hbm] * 14,
        out_specs=(vmem, vmem, vmem),
        scratch_shapes=[
            scratch(BF16, ATOMS, CA),
            scratch(BF16, TOK, COND),
            scratch(BF16, PAIR_ROWS, PAIR_COLS, CA),
            scratch(jnp.int32, 1, TOK),
            scratch(jnp.int32, 1, ATOMS),
            pltpu.SMEM((ATOMS // QB,), jnp.int32),
            scratch(BF16, COND, CA),
            scratch(F32, LAYERS * HEADS, CA),
            scratch(BF16, LAYERS, CA, 4 * CA),
            scratch(BF16, LAYERS, CA, CA),
            scratch(BF16, LAYERS, CA, 2 * FFA),
            scratch(BF16, LAYERS, FFA, CA),
            scratch(BF16, CA, ACT),
            scratch(jnp.int32, 3, 2, ATOMS),
            scratch(BF16, ATOMS, CA),
            scratch(F32, 3, 2, TOK, CA),
            scratch(BF16, 3, 2 * PAIR_PAD, 2 * CA),
            scratch(BF16, 3, 2, TOK, ACT),
            scratch(BF16, CA, ACT),
            scratch(BF16, 3 * ATOMS, CA),
            scratch(F32, 2, ATOMS, CA),
            scratch(BF16, 2, EXT, 2 * CA),
            scratch(BF16, 3 * ATOMS, 2 * CA),
            scratch(F32, LAYERS, EXT, ALL),
            scratch(F32, 3 * HALF, ALL),
            scratch(BF16, 3 * ATOMS, 6 * CA),
            scratch(BF16, LAYERS, CA, CA),
            scratch(BF16, LAYERS, CA, CA),
            scratch(BF16, LAYERS, 2 * FFA, CA),
            scratch(BF16, LAYERS, CA, FFA),
            scratch(F32, LAYERS, EXT, ALL),
            scratch(BF16, LAYERS, EXT, ALL),
            scratch(F32, 3 * HALF, ALL),
            scratch(BF16, ATOMS, ALL),
            scratch(BF16, LAYERS, ALL, CA),
            scratch(BF16, ALL, CA),
            scratch(BF16, LAYERS, CA, EXT),
            scratch(F32, LAYERS, CA, EXT),
            scratch(F32, LAYERS, 1, EXT),
            scratch(F32, LAYERS, CA, EXT),
            scratch(F32, LAYERS, 1, EXT),
            scratch(F32, LAYERS, CA, EXT),
            scratch(F32, LAYERS, CA, ATOMS),
            scratch(F32, LAYERS, FFA, EXT),
            scratch(F32, LAYERS, FFA, EXT),
            scratch(BF16, 2, 2, ATOMS, CA),
            scratch(BF16, 2, 2, ATOMS, CA),
            scratch(BF16, CA, ATOMS),
            scratch(BF16, 2, CA, ATOMS),
            scratch(BF16, 2, TOK, ACT),
            scratch(BF16, 2, TOK, ACT),
            scratch(BF16, 2, TOK, CA),
            scratch(BF16, 2, TOK, CA),
            pltpu.SemaphoreType.DMA((14,)),
            pltpu.SemaphoreType.DMA((N_COPIES,)),
            pltpu.SemaphoreType.DMA((N_COPIES,)),
        ],
        compiler_params=pltpu.CompilerParams(
            collective_id=0, has_side_effects=True, vmem_limit_bytes=64 * 1024 * 1024
        ),
        cost_estimate=pl.CostEstimate(
            flops=2_000_000_000, bytes_accessed=2_000_000, transcendentals=1_000_000
        ),
        name="atoms",
    )(
        atom_single,
        token_single,
        pair_band,
        token_counts.reshape(1, TOK),
        atom_token.reshape(1, ATOMS),
        window_starts,
        single_proj,
        pair_proj.T,
        attn_in,
        attn_out,
        trans_in,
        trans_out,
        agg_proj,
        token_cot,
    )
    return pl.pallas_call(
        hand_on,
        out_shape=results,
        in_specs=[vmem] * 3,
        out_specs=(vmem,) * 3,
        name="results",
    )(*results_here)


def solution(mesh):
    return jax.shard_map(
        local,
        mesh=mesh,
        in_specs=(
            P("seq", None),
            P("seq", "row"),
            P(("seq", "row"), "col", None),
            P("seq"),
            P("seq"),
            P("seq"),
            P("row", None),
            P(),
            P(),
            P(),
            P(),
            P(),
            P(None, "row"),
            P("seq", "row"),
        ),
        out_specs=(P("seq", "row"), P("seq", None), P("seq", "row")),
        check_vma=False,
    )
```

time: 63.8 us -> 45.7 us (0.72)
  the two profiles are of different devices: /device:TPU:1 before, /device:TPU:16 now
where the time goes in v1:
time: 45.7 us; the launch traced here: 45.5 us
  Pallas kernels  44.8 us (98%)
  between operations  0.64 us (1%)
    pallas_call x1, Pallas kernels, local(): pl.pallas_call(kernel, out_shape=results, in_specs=[hbm] * 14, out_specs=...  43.4 us
    pallas_call x1, Pallas kernels, local(): pl.pallas_call(hand_on, out_shape=results, in_specs=[vmem] * 3, out_specs...  1.38 us

profile of v1, /device:TPU:16, one launch (start us, length us, event | category | flops | bytes accessed | tf_op | source)
XLA Modules:
  0.0 45.5 jit_solution(265651828803536349)
XLA Ops:
  0.6 43.4 %atoms.1 = (bf16[16,384]{1,0:T(8,128)(2,1)}, bf16[128,128]{1,0:T(8,128)(2,1)}, bf16[16,192]{1,0:T(8,128)(2,1)}) custom-call(bf16[128,128]{1,0:T(8,128)(2,1)} %atom_hbm.1, bf16[16,192]{1,0:T(8,128)(2,1)} %single_hbm.1, bf16[8,40,128]{2,1,0:T(8,128)(2,1)} %band_hbm.1, s32[1,16]{1,0:T(1,128)} %bitcast.4, s32[1,128]{1,0:T(1,128)} %bitcast.5, s32[4]{0:T(128)} %starts_hbm.1, ...), custom_call_target="tpu_custom_call" | custom-call | flops 2000000000 | bytes 2000000 | tf_op jit(solution)/shard_map/atoms/pallas_call | solution.py:733
  44.1 1.4 %results.1 = (bf16[16,384]{1,0:T(8,128)(2,1)}, bf16[128,128]{1,0:T(8,128)(2,1)}, bf16[16,192]{1,0:T(8,128)(2,1)}) custom-call(bf16[16,384]{1,0:T(8,128)(2,1)} %get-tuple-element.6.act, bf16[128,128]{1,0:T(8,128)(2,1)} %get-tuple-element.7.grad, bf16[16,192]{1,0:T(8,128)(2,1)} %get-tuple-element.8.single), custom_call_target="tpu_custom_call" | custom-call | tf_op jit(solution)/shard_map/results/pallas_call | solution.py:819

commit v2 on v1

--- a/solution.py
+++ b/solution.py
@@ -175,29 +175,53 @@
             lax.rem(col + dc, 2),
         )
 
+    has = {-1: seq > 0, 1: seq < seqs - 1}
+
+    def toward(ds, act):
+        if ds == 0:
+            act()
+        else:
+            pl.when(has[ds])(act)
+
     copies = []
 
-    def send(src, dst, ds, dr=0, dc=0):
-        place = len(copies)
-        copy = pltpu.make_async_remote_copy(
-            src_ref=src,
-            dst_ref=dst,
-            send_sem=send_sem.at[place],
-            recv_sem=recv_sem.at[place],
-            device_id=partner(ds, dr, dc),
-            device_id_type=MESH,
-        )
-        copy.start()
-        copies.append(copy)
-        return copy
+    def send_all(wanted):
+        group = []
+        for src, dst, ds, dr, dc in wanted:
+            place = len(copies)
+            copy = pltpu.make_async_remote_copy(
+                src_ref=src,
+                dst_ref=dst,
+                send_sem=send_sem.at[place],
+                recv_sem=recv_sem.at[place],
+                device_id=partner(ds, dr, dc),
+                device_id_type=MESH,
+            )
+            copies.append((copy, ds))
+            group.append((copy, ds))
+        for side in (-1, 1, 0):
+            mine = [copy for copy, ds in group if ds == side]
+            if mine:
+                toward(side, lambda mine=mine: [copy.start() for copy in mine] and None)
+        return group
 
     def arrive(group):
-        for copy in group:
-            copy.wait_recv()
+        for side in (0, -1, 1):
+            mine = [copy for copy, ds in group if ds == side]
+            if mine:
+                toward(-side, lambda mine=mine: [copy.wait_recv() for copy in mine] and None)
 
     barrier = pltpu.get_barrier_semaphore()
-    for ds, dr, dc in PARTNERS:
-        pl.semaphore_signal(barrier, inc=1, device_id=partner(ds, dr, dc), device_id_type=MESH)
+
+    def greet(side):
+        for ds, dr, dc in PARTNERS:
+            if ds == side:
+                pl.semaphore_signal(
+                    barrier, inc=1, device_id=partner(ds, dr, dc), device_id_type=MESH
+                )
+
+    for side in (-1, 1, 0):
+        toward(side, functools.partial(greet, side))
 
     fetches = []
 
@@ -220,6 +244,31 @@
         fetch(cot_hbm, cot_buf.at[1, 0]),
         fetch(counts_hbm, counts_ref),
     ]
+
+    near, far = pl.ds(0, HALF), pl.ds(HALF, HALF)
+
+    def close(slot, half):
+        id_buf[slot, 0:1] = jnp.full((1, ATOMS), -(2**20), jnp.int32)
+        id_buf[slot, 1:2] = jnp.full((1, ATOMS), 2**20, jnp.int32)
+        cond_buf[slot] = jnp.zeros(cond_buf.shape[1:], F32)
+        pair_buf[slot] = jnp.zeros(pair_buf.shape[1:], BF16)
+        cot_buf[slot] = jnp.zeros(cot_buf.shape[1:], BF16)
+        halo_buf[half] = jnp.zeros((HALF, CA), BF16)
+        for at in (ATOMS, EXT):
+            other = (half.start + at - ATOMS) % ATOMS
+            rows_buf[at + other : at + other + HALF] = jnp.zeros((HALF, CA), BF16)
+        stream_buf[1, half] = jnp.zeros((HALF, CA), F32)
+        opposite = pl.ds(HALF - half.start, HALF)
+        for slot_kv in range(2):
+            for kind in range(2):
+                dkv_recv[slot_kv, kind, opposite] = jnp.zeros((HALF, CA), BF16)
+        side = 1 if slot == 0 else 0
+        part_recv[side] = jnp.zeros((CA, ATOMS), BF16)
+        sums_recv[side] = jnp.zeros((TOK, ACT), BF16)
+        cond_recv[side] = jnp.zeros((TOK, CA), BF16)
+
+    pl.when(seq == 0)(lambda: close(0, far))
+    pl.when(seq == seqs - 1)(lambda: close(2, near))
 
     for copy in first_fetch:
         copy.wait()
@@ -251,30 +300,38 @@
     pair_lanes = pl.ds(pl.multiple_of(row * CA, CA), CA)
     pair_buf[1, pair_rows, pair_lanes] = tile.astype(BF16)
 
-    pl.semaphore_wait(barrier, len(PARTNERS))
-
-    cond_copies = [
-        send(cond_buf.at[1, 0], cond_buf.at[1 - ds, dr], ds, dr) for ds, dr, dc in COND_PARTNERS
-    ]
-    id_copies = [send(id_buf.at[1], id_buf.at[1 - ds], ds) for ds in SIDES]
-    halo_copies = [
-        send(atom_hbm.at[pl.ds(0, HALF)], halo_buf.at[pl.ds(0, HALF)], -1),
-        send(atom_hbm.at[pl.ds(HALF, HALF)], halo_buf.at[pl.ds(HALF, HALF)], 1),
-    ]
-    pair_copies = [
-        send(
-            pair_buf.at[1, pair_rows, pair_lanes],
-            pair_buf.at[1 - ds, pair_rows, pair_lanes],
-            ds,
-            dr,
-            dc,
-        )
-        for ds, dr, dc in PARTNERS
-    ]
-    cot_copies = [
-        send(cot_hbm, cot_buf.at[1 - ds, dr], ds, dr) for ds, dr, dc in COND_PARTNERS
-    ]
-    agg_copy = send(agg_hbm, agg_buf, 0, 1)
+    beyond = len(PARTNERS) // 3 + 1
+    pl.semaphore_wait(
+        barrier, beyond - 1 + beyond * (has[-1].astype(jnp.int32) + has[1].astype(jnp.int32))
+    )
+
+    cond_copies = send_all(
+        [
+            (cond_buf.at[1, 0], cond_buf.at[1 - ds, dr], ds, dr, dc)
+            for ds, dr, dc in COND_PARTNERS
+        ]
+        + [(id_buf.at[1], id_buf.at[1 - ds], ds, 0, 0) for ds in SIDES]
+        + [
+            (atom_hbm.at[near], halo_buf.at[near], -1, 0, 0),
+            (atom_hbm.at[far], halo_buf.at[far], 1, 0, 0),
+        ]
+    )
+    pair_copies = send_all(
+        [
+            (
+                pair_buf.at[1, pair_rows, pair_lanes],
+                pair_buf.at[1 - ds, pair_rows, pair_lanes],
+                ds,
+                dr,
+                dc,
+            )
+            for ds, dr, dc in PARTNERS
+        ]
+    )
+    late_copies = send_all(
+        [(cot_hbm, cot_buf.at[1 - ds, dr], ds, dr, dc) for ds, dr, dc in COND_PARTNERS]
+        + [(agg_hbm, agg_buf, 0, 1, 0)]
+    )
 
     for copy in atom_fetch + weight_fetch:
         copy.wait()
@@ -295,7 +352,7 @@
     own_id_cols = as_cols(own_ids)
     atom_t = flip(atom_ref[...].astype(F32))
 
-    arrive(id_copies + halo_copies + cond_copies)
+    arrive(cond_copies)
     left_ids = id_buf[0, 0:1] - token_base
     right_ids = id_buf[2, 0:1] - token_base
     halo_ids = jnp.where(low, right_ids, left_ids)
@@ -461,20 +518,26 @@
     normal_x[1, :, :ATOMS] = normal
     scale_x[1, :, :ATOMS] = scaling
     rows_buf[:ATOMS] = flip(normal).astype(BF16)
-    lower, upper = pl.ds(0, HALF), pl.ds(HALF, HALF)
-    inner_copies = [
-        send(rows_buf.at[lower], rows_buf.at[pl.ds(ATOMS, HALF)], -1),
-        send(rows_buf.at[upper], rows_buf.at[pl.ds(ATOMS + HALF, HALF)], 1),
-    ]
-    outer_copies = [
-        send(rows_buf.at[upper], rows_buf.at[pl.ds(EXT, HALF)], -1),
-        send(rows_buf.at[lower], rows_buf.at[pl.ds(EXT + HALF, HALF)], 1),
-    ]
+    lower, upper = near, far
+    inner_copies = send_all(
+        [
+            (rows_buf.at[lower], rows_buf.at[pl.ds(ATOMS, HALF)], -1, 0, 0),
+            (rows_buf.at[upper], rows_buf.at[pl.ds(ATOMS + HALF, HALF)], 1, 0, 0),
+        ]
+    )
+    outer_copies = send_all(
+        [
+            (rows_buf.at[upper], rows_buf.at[pl.ds(EXT, HALF)], -1, 0, 0),
+            (rows_buf.at[lower], rows_buf.at[pl.ds(EXT + HALF, HALF)], 1, 0, 0),
+        ]
+    )
     stream_buf[0] = flip(stream)
-    stream_copies = [
-        send(stream_buf.at[0, lower], stream_buf.at[1, lower], -1),
-        send(stream_buf.at[0, upper], stream_buf.at[1, upper], 1),
-    ]
+    stream_copies = send_all(
+        [
+            (stream_buf.at[0, lower], stream_buf.at[1, lower], -1, 0, 0),
+            (stream_buf.at[0, upper], stream_buf.at[1, upper], 1, 0, 0),
+        ]
+    )
     kv_wide[:ATOMS] = nn(rows_buf[:ATOMS], attn_in_ref[1, :, CA : 3 * CA]).astype(BF16)
     q_heads[1] = by_head(nn(rows_buf[:ATOMS], attn_in_ref[1, :, :CA]).astype(BF16).astype(F32))
     bias_layer(1)
@@ -516,7 +579,7 @@
     stream = local_layer(2, stream_ext)
 
     final = flip(stream).astype(BF16)
-    arrive([agg_copy] + cot_copies)
+    arrive(late_copies)
     gradient = None
     for part in range(2):
         weights = agg_ref[...] if part == 0 else agg_buf[...]
@@ -532,9 +595,12 @@
             sums_send[0] = sums[:TOK].astype(BF16)
             sums_send[1] = sums[2 * TOK :].astype(BF16)
             own_sums = sums[TOK : 2 * TOK]
-            sums_copies = [
-                send(sums_send.at[(ds + 1) // 2], sums_recv.at[(ds + 1) // 2], ds) for ds in SIDES
-            ]
+            sums_copies = send_all(
+                [
+                    (sums_send.at[(ds + 1) // 2], sums_recv.at[(ds + 1) // 2], ds, 0, 0)
+                    for ds in SIDES
+                ]
+            )
 
     def d_middle(n, upstream, lanes):
         d_transit = nn(trans_out_ref[n], upstream.astype(BF16))
@@ -592,11 +658,19 @@
 
         def give(kind, values):
             dkv_send[slot, kind] = values.astype(BF16)
-            group.append(
-                send(dkv_send.at[slot, kind, lower], dkv_recv.at[slot, kind, lower], 1)
-            )
-            group.append(
-                send(dkv_send.at[slot, kind, upper], dkv_recv.at[slot, kind, upper], -1)
+            group.extend(
+                send_all(
+                    [
+                        (
+                            dkv_send.at[slot, kind, half],
+                            dkv_recv.at[slot, kind, half],
+                            ds,
+                            0,
+                            0,
+                        )
+                        for half, ds in ((lower, 1), (upper, -1))
+                    ]
+                )
             )
 
         give(1, nn(soft_b[n, ATOMS:], d_att))
@@ -629,7 +703,7 @@
 
     part, group = local_back(2, gradient)
     part_send[...] = part.astype(BF16)
-    part_copies = [send(part_send, part_recv.at[(ds + 1) // 2], ds) for ds in SIDES]
+    part_copies = send_all([(part_send, part_recv.at[(ds + 1) // 2], ds, 0, 0) for ds in SIDES])
     halo_gradient = beside(2)
     arrive(group)
     gradient = part + from_beside(2)
@@ -673,7 +747,9 @@
     d_cond = per_token(pick, part)
     cond_send[0] = d_cond[:TOK].astype(BF16)
     cond_send[1] = d_cond[2 * TOK :].astype(BF16)
-    last_copies = [send(cond_send.at[(ds + 1) // 2], cond_recv.at[(ds + 1) // 2], ds) for ds in SIDES]
+    last_copies = send_all(
+        [(cond_send.at[(ds + 1) // 2], cond_recv.at[(ds + 1) // 2], ds, 0, 0) for ds in SIDES]
+    )
     d_cond = d_cond[TOK : 2 * TOK] + per_token(pick_ext[TOK : 2 * TOK, ATOMS:], beside(0))
     arrive(sums_copies)
     token_sums = own_sums + (sums_recv[0].astype(F32) + sums_recv[1].astype(F32))
@@ -690,8 +766,10 @@
     d_cond = d_cond + (cond_recv[0].astype(F32) + cond_recv[1].astype(F32))
     high, rest = split(d_cond)
     single_out[...] = (nt(high, proj_ref[...]) + nt(rest, proj_ref[...])).astype(BF16)
-    for copy in copies:
-        copy.wait_send()
+    for side in (0, -1, 1):
+        toward(
+            side, lambda side=side: [copy.wait_send() for copy, ds in copies if ds == side] and None
+        )
 
 
 N_COPIES = 5 + 2 + 2 + 11 + 5 + 1 + 6 + 2 + 4 + 2 + 4 + 2

time: 45.7 us -> 39.6 us (0.87)
  the two profiles are of different devices: /device:TPU:16 before, /device:TPU:384 now
where the time goes in v2:
time: 39.6 us; the launch traced here: 39.4 us
  Pallas kernels  38.8 us (98%)
  between operations  0.64 us (2%)
    pallas_call x1, Pallas kernels, local(): pl.pallas_call(kernel, out_shape=results, in_specs=[hbm] * 14, out_specs=...  37.4 us
    pallas_call x1, Pallas kernels, local(): pl.pallas_call(hand_on, out_shape=results, in_specs=[vmem] * 3, out_specs...  1.38 us

profile of v2, /device:TPU:384, one launch (start us, length us, event | category | flops | bytes accessed | tf_op | source)
XLA Modules:
  0.0 39.4 jit_solution(3174754476335295697)
XLA Ops:
  0.6 37.4 %atoms.1 = (bf16[16,384]{1,0:T(8,128)(2,1)}, bf16[128,128]{1,0:T(8,128)(2,1)}, bf16[16,192]{1,0:T(8,128)(2,1)}) custom-call(bf16[128,128]{1,0:T(8,128)(2,1)} %atom_hbm.1, bf16[16,192]{1,0:T(8,128)(2,1)} %single_hbm.1, bf16[8,40,128]{2,1,0:T(8,128)(2,1)} %band_hbm.1, s32[1,16]{1,0:T(1,128)} %bitcast.4, s32[1,128]{1,0:T(1,128)} %bitcast.5, s32[4]{0:T(128)} %starts_hbm.1, ...), custom_call_target="tpu_custom_call" | custom-call | flops 2000000000 | bytes 2000000 | tf_op jit(solution)/shard_map/atoms/pallas_call | solution.py:811
  38.0 1.4 %results.1 = (bf16[16,384]{1,0:T(8,128)(2,1)}, bf16[128,128]{1,0:T(8,128)(2,1)}, bf16[16,192]{1,0:T(8,128)(2,1)}) custom-call(bf16[16,384]{1,0:T(8,128)(2,1)} %get-tuple-element.6.act, bf16[128,128]{1,0:T(8,128)(2,1)} %get-tuple-element.7.grad, bf16[16,192]{1,0:T(8,128)(2,1)} %get-tuple-element.8.single), custom_call_target="tpu_custom_call" | custom-call | tf_op jit(solution)/shard_map/results/pallas_call | solution.py:897

commit v3 on v2

--- a/solution.py
+++ b/solution.py
@@ -75,10 +75,18 @@
     )
 
 
-def by_head(rows):
-    head = iota(rows.shape, 1) // (CA // HEADS)
+def by_head(columns):
+    width = CA // HEADS
+    none = jnp.zeros((width, columns.shape[1]), BF16)
     return jnp.concatenate(
-        [jnp.where(head == h, rows, 0.0).astype(BF16) for h in range(HEADS)], axis=0
+        [
+            jnp.concatenate(
+                [columns[width * h : width * (h + 1)] if g == h else none for g in range(HEADS)],
+                axis=0,
+            )
+            for h in range(HEADS)
+        ],
+        axis=1,
     )
 
 
@@ -130,7 +138,8 @@
     kv_wide,
     bias,
     bias_rim,
-    mixed,
+    takes,
+    query_t,
     gate_t,
     out_t,
     in_t,
@@ -150,14 +159,11 @@
     gate_back,
     silu_a,
     back_a,
-    dkv_send,
-    dkv_recv,
-    part_send,
-    part_recv,
+    own_picks,
+    edge_send,
+    edge_recv,
     sums_send,
     sums_recv,
-    cond_send,
-    cond_recv,
     local_sem,
     send_sem,
     recv_sem,
@@ -184,6 +190,16 @@
             pl.when(has[ds])(act)
 
     copies = []
+
+    def each(group, side, source, act):
+        mine = [copy for copy, ds in group if ds == side]
+
+        def run():
+            for copy in mine:
+                act(copy)
+
+        if mine:
+            toward(source, run)
 
     def send_all(wanted):
         group = []
@@ -200,16 +216,22 @@
             copies.append((copy, ds))
             group.append((copy, ds))
         for side in (-1, 1, 0):
-            mine = [copy for copy, ds in group if ds == side]
-            if mine:
-                toward(side, lambda mine=mine: [copy.start() for copy in mine] and None)
+            each(group, side, side, lambda copy: copy.start())
         return group
 
     def arrive(group):
         for side in (0, -1, 1):
-            mine = [copy for copy, ds in group if ds == side]
-            if mine:
-                toward(-side, lambda mine=mine: [copy.wait_recv() for copy in mine] and None)
+            each(group, side, -side, lambda copy: copy.wait_recv())
+
+    fetches = []
+
+    def fetch(src, dst):
+        copy = pltpu.make_async_copy(src, dst, local_sem.at[len(fetches)])
+        copy.start()
+        fetches.append(copy)
+        return copy
+
+    first_fetch = [fetch(single_hbm, single_ref), fetch(proj_hbm, proj_ref)]
 
     barrier = pltpu.get_barrier_semaphore()
 
@@ -223,15 +245,6 @@
     for side in (-1, 1, 0):
         toward(side, functools.partial(greet, side))
 
-    fetches = []
-
-    def fetch(src, dst):
-        copy = pltpu.make_async_copy(src, dst, local_sem.at[len(fetches)])
-        copy.start()
-        fetches.append(copy)
-        return copy
-
-    first_fetch = [fetch(single_hbm, single_ref), fetch(proj_hbm, proj_ref)]
     pair_fetch = [fetch(band_hbm, band_ref), fetch(pair_proj_hbm, pair_proj_ref)]
     id_fetch = [fetch(ids_hbm, ids_ref), fetch(starts_hbm, starts_ref)]
     atom_fetch = [fetch(atom_hbm, atom_ref)]
@@ -258,14 +271,10 @@
             other = (half.start + at - ATOMS) % ATOMS
             rows_buf[at + other : at + other + HALF] = jnp.zeros((HALF, CA), BF16)
         stream_buf[1, half] = jnp.zeros((HALF, CA), F32)
-        opposite = pl.ds(HALF - half.start, HALF)
-        for slot_kv in range(2):
-            for kind in range(2):
-                dkv_recv[slot_kv, kind, opposite] = jnp.zeros((HALF, CA), BF16)
         side = 1 if slot == 0 else 0
-        part_recv[side] = jnp.zeros((CA, ATOMS), BF16)
+        for back in range(2):
+            edge_recv[back, side] = jnp.zeros((CA, ATOMS), BF16)
         sums_recv[side] = jnp.zeros((TOK, ACT), BF16)
-        cond_recv[side] = jnp.zeros((TOK, CA), BF16)
 
     pl.when(seq == 0)(lambda: close(0, far))
     pl.when(seq == seqs - 1)(lambda: close(2, near))
@@ -328,14 +337,10 @@
             for ds, dr, dc in PARTNERS
         ]
     )
-    late_copies = send_all(
-        [(cot_hbm, cot_buf.at[1 - ds, dr], ds, dr, dc) for ds, dr, dc in COND_PARTNERS]
-        + [(agg_hbm, agg_buf, 0, 1, 0)]
-    )
-
     for copy in atom_fetch + weight_fetch:
         copy.wait()
     for n in range(LAYERS):
+        query_t[n] = flip(attn_in_ref[n, :, :CA])
         gate_t[n] = flip(attn_in_ref[n, :, 3 * CA :])
         out_t[n] = flip(attn_out_ref[n])
         in_t[n] = flip(trans_in_ref[n])
@@ -350,7 +355,7 @@
 
     own_ids = ids_ref[...] - token_base
     own_id_cols = as_cols(own_ids)
-    atom_t = flip(atom_ref[...].astype(F32))
+    atom_t = flip(atom_ref[...]).astype(F32)
 
     arrive(cond_copies)
     left_ids = id_buf[0, 0:1] - token_base
@@ -362,8 +367,8 @@
     ).astype(BF16)
     pick = pick_ext[:, :ATOMS]
     cond = (cond_buf[:, 0] + cond_buf[:, 1]).astype(BF16).reshape(SPAN, CA)
-    cond_t = flip(cond.astype(F32)).astype(BF16)
-    stream_ext = jnp.concatenate([atom_t, flip(halo_buf[...].astype(F32))], axis=1) + nn(
+    cond_t = flip(cond)
+    stream_ext = jnp.concatenate([atom_t, flip(halo_buf[...]).astype(F32)], axis=1) + nn(
         cond_t, pick_ext
     )
 
@@ -373,37 +378,55 @@
     outside = jnp.where((position >= first) & (position < first + KW), 0.0, -1e30)
     outside = jnp.concatenate([outside] * HEADS, axis=1)
 
-    wide = 3 * 2 * CA
-    place = iota((wide, ATOMS), 0)
-    head_of = (place // PAIR_ROWS) % (CA // PAIR_ROWS)
-    token_of = TOK * (place // (2 * CA)) + PAIR_ROWS * ((place // CA) % 2) + place % PAIR_ROWS
-
-    def mix_bias(at, id_cols):
-        rows = id_cols.shape[0]
-        lanes = iota((rows, 2 * PAIR_PAD), 1)
+    place = iota((2 * CA, ATOMS), 0)
+    head_of = (place // PAIR_ROWS) % HEADS
+    token_of = PAIR_ROWS * (place // (PAIR_ROWS * HEADS)) + place % PAIR_ROWS
+
+    def take_of(id_cols):
+        lanes = iota((id_cols.shape[0], CA), 1)
         column = jnp.where(
             lanes < PAIR_PAD,
             jnp.where(lanes < PAIR_COLS, lanes, -4096),
             jnp.where(lanes < PAIR_PAD + PAIR_COLS, lanes - (PAIR_PAD - PAIR_COLS), -4096),
         )
+        return jnp.concatenate(
+            [
+                (id_cols + (2 - s) * TOK == column).astype(F32).astype(BF16)
+                for s in range(3)
+            ],
+            axis=1,
+        )
+
+    def table_of(n):
+        part = PAIR_ROWS * HEADS
+        none = jnp.zeros((CA, CA), BF16)
+        blocks = []
         for s in range(3):
-            take = (id_cols[:, : 2 * PAIR_PAD] + (2 - s) * TOK == column).astype(F32).astype(BF16)
-            mixed[at : at + rows, 2 * CA * s : 2 * CA * (s + 1)] = nn(take, pair_buf[s]).astype(
-                BF16
-            )
-
-    def bias_picks(n, ids):
+            at = 2 * part * (s % 2)
+            here = pair_buf[s].astype(F32)
+            halves = []
+            for r in range(2):
+                shift = (at + part * r - part * n) % CA
+                half = here[:, CA * r : CA * (r + 1)]
+                halves.append(pltpu.roll(half, shift, 1) if shift else half)
+            inside = lane - at
+            piece = jnp.where(
+                (inside >= 0) & (inside < part),
+                halves[0],
+                jnp.where((inside >= part) & (inside < 2 * part), halves[1], 0.0),
+            ).astype(BF16)
+            piece = jnp.concatenate([piece, none[: CA - 2 * PAIR_PAD]], axis=0)
+            blocks.append(jnp.concatenate([piece, none] if s < 2 else [none, piece], axis=1))
+        return jnp.concatenate(blocks, axis=0)
+
+    def bias_picks(ids):
         hit = token_of == ids
         return jnp.concatenate(
-            [
-                (hit & (head_of == HEADS * n + h)).astype(F32).astype(BF16)
-                for h in range(HEADS)
-            ],
-            axis=1,
-        )
-
-    def bias_layer(n):
-        bias[n] = nn(mixed[:EXT], bias_picks(n, own_ids)) + outside
+            [(hit & (head_of == h)).astype(F32).astype(BF16) for h in range(HEADS)], axis=1
+        )
+
+    def bias_of(taken, n, picks):
+        return nn(nn(taken, table_of(n)).astype(BF16), picks)
 
     def right_rows(values):
         return jnp.concatenate(
@@ -417,44 +440,31 @@
 
     low_all = jnp.concatenate([low] * HEADS, axis=1)
 
-    def attend_own(n, kv_n, wait_for):
-        own_scores = nt(kv_n[:ATOMS, :CA], q_heads[n]) * SCALE + bias[n, :ATOMS]
-        own_values = flip(kv_n[:ATOMS, CA:])
-        arrive(wait_for)
-        halo_scores = nt(kv_n[ATOMS:EXT, :CA], q_heads[n]) * SCALE + bias[n, ATOMS:]
-        halo_values = flip(kv_n[ATOMS:EXT, CA:])
-        most = jnp.maximum(
-            jnp.max(own_scores, axis=0, keepdims=True), jnp.max(halo_scores, axis=0, keepdims=True)
-        )
-        own_exp = jnp.exp(own_scores - most)
-        halo_exp = jnp.exp(halo_scores - most)
-        total = jnp.sum(own_exp, axis=0, keepdims=True) + jnp.sum(halo_exp, axis=0, keepdims=True)
-        share = 1.0 / total
-        own_soft = own_exp * share
-        halo_soft = halo_exp * share
-        soft[n, :ATOMS] = own_soft
-        soft[n, ATOMS:] = halo_soft
-        soft_b[n, :ATOMS] = own_soft.astype(BF16)
-        soft_b[n, ATOMS:] = halo_soft.astype(BF16)
-        values_t = jnp.concatenate([own_values, halo_values], axis=1)
-        key_t[n, :, :ATOMS] = flip(kv_n[:ATOMS, :CA])
-        key_t[n, :, ATOMS:] = flip(kv_n[ATOMS:EXT, :CA])
+    def attend_own(n, kv_n, heads):
+        scores = nn(kv_n[:EXT, :CA], heads) * SCALE + bias[n]
+        values_t = flip(kv_n[:EXT, CA:])
+        exps = jnp.exp(scores - jnp.max(scores, axis=0, keepdims=True))
+        weights = exps * (1.0 / jnp.sum(exps, axis=0, keepdims=True))
+        rounded = weights.astype(BF16)
+        soft[n] = weights
+        soft_b[n] = rounded
+        key_t[n] = flip(kv_n[:EXT, :CA])
         return jnp.concatenate(
             [
                 nn(
                     values_t[width * h : width * (h + 1)],
-                    soft_b[n, :, ATOMS * h : ATOMS * (h + 1)],
+                    rounded[:, ATOMS * h : ATOMS * (h + 1)],
                 )
                 for h in range(HEADS)
             ],
             axis=0,
         )
 
-    def attend_rim(n, kv_n):
+    def attend_rim(n, kv_n, heads):
         right_kv = right_rows(kv_n)
         left_kv = left_rows(kv_n)
         scores = jnp.where(
-            low_all, nt(right_kv[:, :CA], q_rim[...]), nt(left_kv[:, :CA], q_rim[...])
+            low_all, nn(right_kv[:, :CA], heads), nn(left_kv[:, :CA], heads)
         )
         scores = scores * SCALE + bias_rim[...]
         most = jnp.maximum(jnp.max(scores, axis=0, keepdims=True), -1e29)
@@ -500,16 +510,18 @@
         normal_ext, scale_ext = norm_rows(stream_ext)
         normal_x[n] = normal_ext
         scale_x[n] = scale_ext
-        rows_ext = flip(normal_ext).astype(BF16)
+        rows_ext = flip(normal_ext.astype(BF16))
         kv[n // 2] = nn(rows_ext, attn_in_ref[n, :, CA : 3 * CA]).astype(BF16)
-        queries = nn(rows_ext[:ATOMS], attn_in_ref[n, :, :CA]).astype(BF16).astype(F32)
-        q_heads[n] = by_head(queries)
-        gates = jax.nn.sigmoid(nn(gate_t[n], normal_ext[:, :ATOMS].astype(BF16)))
+        normed = normal_ext[:, :ATOMS].astype(BF16)
+        heads = by_head(nn(query_t[n], normed).astype(BF16))
+        q_heads[n] = flip(heads)
+        gates = jax.nn.sigmoid(nn(gate_t[n], normed))
         if n == 0:
+            own_picks[...] = bias_picks(own_ids)
+            takes[:EXT] = take_of(jnp.concatenate([own_id_cols, halo_id_cols], axis=0))
             arrive(pair_copies)
-            mix_bias(0, jnp.concatenate([own_id_cols, halo_id_cols], axis=0))
-            bias_layer(n)
-        attended = attend_own(n, kv[n // 2], [])
+            bias[0] = bias_of(takes[:EXT], 0, own_picks[...]) + outside
+        attended = attend_own(n, kv[n // 2], heads)
         return transition(n, stream_ext[:, :ATOMS], gates, attended, ATOMS)
 
     stream = local_layer(0, stream_ext)
@@ -517,7 +529,7 @@
     normal, scaling = norm_rows(stream)
     normal_x[1, :, :ATOMS] = normal
     scale_x[1, :, :ATOMS] = scaling
-    rows_buf[:ATOMS] = flip(normal).astype(BF16)
+    rows_buf[:ATOMS] = flip(normal.astype(BF16))
     lower, upper = near, far
     inner_copies = send_all(
         [
@@ -538,12 +550,19 @@
             (stream_buf.at[0, upper], stream_buf.at[1, upper], 1, 0, 0),
         ]
     )
+    late_copies = send_all(
+        [(cot_hbm, cot_buf.at[1 - ds, dr], ds, dr, dc) for ds, dr, dc in COND_PARTNERS]
+        + [(agg_hbm, agg_buf, 0, 1, 0)]
+    )
+
     kv_wide[:ATOMS] = nn(rows_buf[:ATOMS], attn_in_ref[1, :, CA : 3 * CA]).astype(BF16)
-    q_heads[1] = by_head(nn(rows_buf[:ATOMS], attn_in_ref[1, :, :CA]).astype(BF16).astype(F32))
-    bias_layer(1)
+    heads = by_head(nn(query_t[1], normal.astype(BF16)).astype(BF16))
+    q_heads[1] = flip(heads)
     outer_ids = pltpu.roll(jnp.where(low, left_ids, right_ids), HALF, 1)
-    mix_bias(EXT, as_cols(outer_ids))
-    rim_full = nn(mixed[...], bias_picks(1, halo_ids))
+    takes[EXT:] = take_of(as_cols(outer_ids))
+    mixed = nn(takes[...], table_of(1)).astype(BF16)
+    bias[1] = nn(mixed[:EXT], own_picks[...]) + outside
+    rim_full = nn(mixed, bias_picks(halo_ids))
     rim_rows = iota((3 * HALF, ATOMS), 0)
     left_position = jnp.where(
         rim_rows < HALF,
@@ -558,7 +577,7 @@
     bias_rim[...] = jnp.where(low_all, right_rows(rim_full), left_rows(rim_full)) + jnp.concatenate(
         [rim_outside] * HEADS, axis=1
     )
-    bias_layer(2)
+    bias[2] = bias_of(takes[:EXT], 2, own_picks[...]) + outside
     at_token = jnp.concatenate([own_id_cols, halo_id_cols], axis=0) == iota((EXT, CA), 1)
     pick_t = at_token[:ATOMS].astype(F32).astype(BF16)[:, :SPAN]
     token_atoms = jnp.sum(at_token.astype(F32), axis=0, keepdims=True)
@@ -566,19 +585,20 @@
     inverse = 1.0 / jnp.maximum(atom_counts, 1.0)
     arrive(inner_copies)
     kv_wide[ATOMS:EXT] = nn(rows_buf[ATOMS:EXT], attn_in_ref[1, :, CA : 3 * CA]).astype(BF16)
-    attended = attend_own(1, kv_wide, [])
+    attended = attend_own(1, kv_wide, heads)
     gates = jax.nn.sigmoid(nt(gate_t[1], rows_buf[:EXT]))
-    q_rim[...] = by_head(nn(rows_buf[ATOMS:EXT], attn_in_ref[1, :, :CA]).astype(BF16).astype(F32))
+    heads = by_head(nt(query_t[1], rows_buf[ATOMS:EXT]).astype(BF16))
+    q_rim[...] = flip(heads)
     arrive(outer_copies)
     kv_wide[EXT:] = nn(rows_buf[EXT:], attn_in_ref[1, :, CA : 3 * CA]).astype(BF16)
-    attended = jnp.concatenate([attended, attend_rim(1, kv_wide)], axis=1)
+    attended = jnp.concatenate([attended, attend_rim(1, kv_wide, heads)], axis=1)
     arrive(stream_copies)
     stream_ext = jnp.concatenate([stream, flip(stream_buf[1])], axis=1)
     stream_ext = transition(1, stream_ext, gates, attended, EXT)
 
     stream = local_layer(2, stream_ext)
 
-    final = flip(stream).astype(BF16)
+    final = flip(stream.astype(BF16))
     arrive(late_copies)
     gradient = None
     for part in range(2):
@@ -616,9 +636,9 @@
         )
         return d_mid, nn(attn_out_ref[n], d_mid.astype(BF16))
 
-    def d_own(n, kv_n, d_att, sent):
-        own_d = nt(kv_n[:ATOMS, CA:], d_att)
-        halo_d = nt(kv_n[ATOMS:EXT, CA:], d_att)
+    def d_own(n, kv_n, d_heads, d_att):
+        own_d = nn(kv_n[:ATOMS, CA:], d_heads)
+        halo_d = nn(kv_n[ATOMS:EXT, CA:], d_heads)
         own_prod = soft[n, :ATOMS] * own_d
         halo_prod = soft[n, ATOMS:] * halo_d
         inner = jnp.sum(own_prod, axis=0, keepdims=True) + jnp.sum(
@@ -626,8 +646,6 @@
         )
         halo_ds = ((halo_prod - soft[n, ATOMS:] * inner) * SCALE).astype(BF16)
         own_ds = ((own_prod - soft[n, :ATOMS] * inner) * SCALE).astype(BF16)
-        if sent is not None:
-            sent(halo_ds)
         d_queries = jnp.concatenate(
             [
                 nn(
@@ -642,7 +660,7 @@
             ],
             axis=0,
         ).astype(BF16)
-        return d_queries, nn(own_ds, q_heads[n]), nn(soft_b[n, :ATOMS], d_att)
+        return d_queries, nn(own_ds, q_heads[n]), nn(soft_b[n, :ATOMS], d_att), halo_ds
 
     def weigh_kv(n, d_keys, d_vals):
         return nt(attn_in_ref[n, :, CA : 2 * CA], d_keys) + nt(
@@ -652,30 +670,18 @@
     def local_back(n, upstream):
         slot = n // 2
         d_mid, d_gated = d_middle(n, upstream, ATOMS)
-        d_att = by_head(flip(d_gated * gating[n, :, :ATOMS]))
+        d_heads = by_head((d_gated * gating[n, :, :ATOMS]).astype(BF16))
+        d_att = flip(d_heads)
         d_gate = (d_gated * gate_back[n]).astype(BF16)
-        group = []
-
-        def give(kind, values):
-            dkv_send[slot, kind] = values.astype(BF16)
-            group.extend(
-                send_all(
-                    [
-                        (
-                            dkv_send.at[slot, kind, half],
-                            dkv_recv.at[slot, kind, half],
-                            ds,
-                            0,
-                            0,
-                        )
-                        for half, ds in ((lower, 1), (upper, -1))
-                    ]
-                )
-            )
-
-        give(1, nn(soft_b[n, ATOMS:], d_att))
-        d_queries, d_keys, d_vals = d_own(
-            n, kv[slot], d_att, lambda halo_ds: give(0, nn(halo_ds, q_heads[n]))
+        d_queries, d_keys, d_vals, halo_ds = d_own(n, kv[slot], d_heads, d_att)
+        beside = norm_back(
+            normal_x[n, :, ATOMS:],
+            scale_x[n, :, ATOMS:],
+            weigh_kv(
+                n,
+                nn(halo_ds, q_heads[n]).astype(BF16),
+                nn(soft_b[n, ATOMS:], d_att).astype(BF16),
+            ),
         )
         d_normed = (
             nn(attn_in_ref[n, :, :CA], d_queries)
@@ -683,44 +689,39 @@
             + weigh_kv(n, d_keys.astype(BF16), d_vals.astype(BF16))
         )
         part = d_mid + norm_back(normal_x[n, :, :ATOMS], scale_x[n, :, :ATOMS], d_normed)
-        return part, group
-
-    def beside(n):
-        slot = n // 2
-        return norm_back(
-            normal_x[n, :, ATOMS:],
-            scale_x[n, :, ATOMS:],
-            weigh_kv(n, dkv_send[slot, 0], dkv_send[slot, 1]),
-        )
-
-    def from_beside(n):
-        slot = n // 2
-        return norm_back(
-            normal_x[n, :, :ATOMS],
-            scale_x[n, :, :ATOMS],
-            weigh_kv(n, dkv_recv[slot, 0], dkv_recv[slot, 1]),
-        )
-
-    part, group = local_back(2, gradient)
-    part_send[...] = part.astype(BF16)
-    part_copies = send_all([(part_send, part_recv.at[(ds + 1) // 2], ds, 0, 0) for ds in SIDES])
-    halo_gradient = beside(2)
-    arrive(group)
-    gradient = part + from_beside(2)
-    arrive(part_copies)
-    halo_gradient = halo_gradient + jnp.where(low, part_recv[0], part_recv[1]).astype(F32)
-    gradient = jnp.concatenate([gradient, halo_gradient], axis=1)
+        edge_send[slot, 0] = jnp.where(low, part, beside).astype(BF16)
+        edge_send[slot, 1] = jnp.where(low, beside, part).astype(BF16)
+        arrive(
+            send_all(
+                [
+                    (edge_send.at[slot, side], edge_recv.at[slot, side], ds, 0, 0)
+                    for side, ds in enumerate(SIDES)
+                ]
+            )
+        )
+        from_right, from_left = edge_recv[slot, 0].astype(F32), edge_recv[slot, 1].astype(F32)
+        return jnp.concatenate(
+            [
+                part + jnp.where(low, from_left, from_right),
+                beside + jnp.where(low, from_right, from_left),
+            ],
+            axis=1,
+        )
+
+    gradient = local_back(2, gradient)
 
     d_mid, d_gated = d_middle(1, gradient, EXT)
-    d_att_t = d_gated * gating[1]
-    d_att = by_head(flip(d_att_t[:, :ATOMS]))
-    d_att_rim = by_head(flip(d_att_t[:, ATOMS:]))
+    d_att_t = (d_gated * gating[1]).astype(BF16)
+    d_heads = by_head(d_att_t[:, :ATOMS])
+    d_att = flip(d_heads)
+    d_heads_rim = by_head(d_att_t[:, ATOMS:])
+    d_att_rim = flip(d_heads_rim)
     d_gate = (d_gated[:, :ATOMS] * gate_back[1]).astype(BF16)
-    d_queries, d_keys, d_vals = d_own(1, kv_wide, d_att, None)
+    d_queries, d_keys, d_vals, _ = d_own(1, kv_wide, d_heads, d_att)
     rim_d = jnp.where(
         low_all,
-        nt(right_rows(kv_wide[:, CA:]), d_att_rim),
-        nt(left_rows(kv_wide[:, CA:]), d_att_rim),
+        nn(right_rows(kv_wide[:, CA:]), d_heads_rim),
+        nn(left_rows(kv_wide[:, CA:]), d_heads_rim),
     )
     rim_prod = soft_rim[...] * rim_d
     rim_inner = jnp.sum(rim_prod, axis=0, keepdims=True)
@@ -743,14 +744,6 @@
         high, rest = split(values)
         return nt(picks, high) + nt(picks, rest)
 
-    part, group = local_back(0, gradient)
-    d_cond = per_token(pick, part)
-    cond_send[0] = d_cond[:TOK].astype(BF16)
-    cond_send[1] = d_cond[2 * TOK :].astype(BF16)
-    last_copies = send_all(
-        [(cond_send.at[(ds + 1) // 2], cond_recv.at[(ds + 1) // 2], ds, 0, 0) for ds in SIDES]
-    )
-    d_cond = d_cond[TOK : 2 * TOK] + per_token(pick_ext[TOK : 2 * TOK, ATOMS:], beside(0))
     arrive(sums_copies)
     token_sums = own_sums + (sums_recv[0].astype(F32) + sums_recv[1].astype(F32))
     diagonal = iota((TOK, TOK), 0) == iota((TOK, TOK), 1)
@@ -758,21 +751,16 @@
         jnp.where(diagonal, counts_ref[...].astype(F32), 0.0), axis=1, keepdims=True
     )
     act_out[...] = (token_sums / counts).astype(BF16)
-    arrive(group)
-    rest_gradient = from_beside(0)
-    grad_out[...] = flip(part + rest_gradient).astype(BF16)
-    d_cond = d_cond + per_token(pick[TOK : 2 * TOK], rest_gradient)
-    arrive(last_copies)
-    d_cond = d_cond + (cond_recv[0].astype(F32) + cond_recv[1].astype(F32))
+    gradient = local_back(0, gradient)
+    grad_out[...] = flip(gradient[:, :ATOMS].astype(BF16))
+    d_cond = per_token(pick_ext[TOK : 2 * TOK], gradient)
     high, rest = split(d_cond)
     single_out[...] = (nt(high, proj_ref[...]) + nt(rest, proj_ref[...])).astype(BF16)
     for side in (0, -1, 1):
-        toward(
-            side, lambda side=side: [copy.wait_send() for copy, ds in copies if ds == side] and None
-        )
-
-
-N_COPIES = 5 + 2 + 2 + 11 + 5 + 1 + 6 + 2 + 4 + 2 + 4 + 2
+        each(copies, side, side, lambda copy: copy.wait_send())
+
+
+N_COPIES = 5 + 2 + 2 + 11 + 5 + 1 + 6 + 2 + 2 + 2
 
 
 def hand_on(act, grad, single, act_out, grad_out, single_out):
@@ -839,7 +827,8 @@
             scratch(BF16, 3 * ATOMS, 2 * CA),
             scratch(F32, LAYERS, EXT, ALL),
             scratch(F32, 3 * HALF, ALL),
-            scratch(BF16, 3 * ATOMS, 6 * CA),
+            scratch(BF16, 3 * ATOMS, 3 * CA),
+            scratch(BF16, LAYERS, CA, CA),
             scratch(BF16, LAYERS, CA, CA),
             scratch(BF16, LAYERS, CA, CA),
             scratch(BF16, LAYERS, 2 * FFA, CA),
@@ -859,14 +848,11 @@
             scratch(F32, LAYERS, CA, ATOMS),
             scratch(F32, LAYERS, FFA, EXT),
             scratch(F32, LAYERS, FFA, EXT),
-            scratch(BF16, 2, 2, ATOMS, CA),
-            scratch(BF16, 2, 2, ATOMS, CA),
-            scratch(BF16, CA, ATOMS),
-            scratch(BF16, 2, CA, ATOMS),
+            scratch(BF16, 2 * CA, ALL),
+            scratch(BF16, 2, 2, CA, ATOMS),
+            scratch(BF16, 2, 2, CA, ATOMS),
             scratch(BF16, 2, TOK, ACT),
             scratch(BF16, 2, TOK, ACT),
-            scratch(BF16, 2, TOK, CA),
-            scratch(BF16, 2, TOK, CA),
             pltpu.SemaphoreType.DMA((14,)),
             pltpu.SemaphoreType.DMA((N_COPIES,)),
             pltpu.SemaphoreType.DMA((N_COPIES,)),

time: 39.6 us -> 39 us (0.985)
  Pallas kernels: 38.8 us -> 38.2 us
    pallas_call x1, Pallas kernels: 37.4 us -> 36.8 us  [local(): pl.pallas_call(kernel, out_shape=results, in_specs=[hbm] * 14, out_specs=...]
where the time goes in v3:
time: 39 us; the launch traced here: 38.8 us
  Pallas kernels  38.2 us (98%)
  between operations  0.64 us (2%)
    pallas_call x1, Pallas kernels, local(): pl.pallas_call(kernel, out_shape=results, in_specs=[hbm] * 14, out_specs=...  36.8 us
    pallas_call x1, Pallas kernels, local(): pl.pallas_call(hand_on, out_shape=results, in_specs=[vmem] * 3, out_specs...  1.38 us

profile of v3, /device:TPU:384, one launch (start us, length us, event | category | flops | bytes accessed | tf_op | source)
XLA Modules:
  0.0 38.8 jit_solution(6067511314207141359)
XLA Ops:
  0.6 36.8 %atoms.1 = (bf16[16,384]{1,0:T(8,128)(2,1)}, bf16[128,128]{1,0:T(8,128)(2,1)}, bf16[16,192]{1,0:T(8,128)(2,1)}) custom-call(bf16[128,128]{1,0:T(8,128)(2,1)} %atom_hbm.1, bf16[16,192]{1,0:T(8,128)(2,1)} %single_hbm.1, bf16[8,40,128]{2,1,0:T(8,128)(2,1)} %band_hbm.1, s32[1,16]{1,0:T(1,128)} %bitcast.4, s32[1,128]{1,0:T(1,128)} %bitcast.5, s32[4]{0:T(128)} %starts_hbm.1, ...), custom_call_target="tpu_custom_call" | custom-call | flops 2000000000 | bytes 2000000 | tf_op jit(solution)/shard_map/atoms/pallas_call | solution.py:799
  37.5 1.4 %results.1 = (bf16[16,384]{1,0:T(8,128)(2,1)}, bf16[128,128]{1,0:T(8,128)(2,1)}, bf16[16,192]{1,0:T(8,128)(2,1)}) custom-call(bf16[16,384]{1,0:T(8,128)(2,1)} %get-tuple-element.6.act, bf16[128,128]{1,0:T(8,128)(2,1)} %get-tuple-element.7.grad, bf16[16,192]{1,0:T(8,128)(2,1)} %get-tuple-element.8.single), custom_call_target="tpu_custom_call" | custom-call | tf_op jit(solution)/shard_map/results/pallas_call | solution.py:883

commit v4 on v3

--- a/solution.py
+++ b/solution.py
@@ -32,13 +32,15 @@
 
 PARTNERS = [
     (ds, dr, dc)
-    for ds in (0, -1, 1)
+    for ds in (0, -1, 1, -2, 2)
     for dr in (0, 1)
     for dc in (0, 1)
     if (ds, dr, dc) != (0, 0, 0)
 ]
 COND_PARTNERS = [p for p in PARTNERS if p[2] == 0]
 SIDES = (-1, 1)
+REACH = 2
+SLOTS = 2 * REACH + 1
 
 
 def nn(a, b):
@@ -132,8 +134,8 @@
     pair_buf,
     cot_buf,
     agg_buf,
-    rows_buf,
-    stream_buf,
+    atom_buf,
+    kv_side,
     kv,
     kv_wide,
     bias,
@@ -181,7 +183,7 @@
             lax.rem(col + dc, 2),
         )
 
-    has = {-1: seq > 0, 1: seq < seqs - 1}
+    has = {-1: seq > 0, 1: seq < seqs - 1, -2: seq > 1, 2: seq < seqs - 2}
 
     def toward(ds, act):
         if ds == 0:
@@ -215,23 +217,13 @@
             )
             copies.append((copy, ds))
             group.append((copy, ds))
-        for side in (-1, 1, 0):
+        for side in (-1, 1, -2, 2, 0):
             each(group, side, side, lambda copy: copy.start())
         return group
 
     def arrive(group):
-        for side in (0, -1, 1):
+        for side in (0, -1, 1, -2, 2):
             each(group, side, -side, lambda copy: copy.wait_recv())
-
-    fetches = []
-
-    def fetch(src, dst):
-        copy = pltpu.make_async_copy(src, dst, local_sem.at[len(fetches)])
-        copy.start()
-        fetches.append(copy)
-        return copy
-
-    first_fetch = [fetch(single_hbm, single_ref), fetch(proj_hbm, proj_ref)]
 
     barrier = pltpu.get_barrier_semaphore()
 
@@ -242,9 +234,18 @@
                     barrier, inc=1, device_id=partner(ds, dr, dc), device_id_type=MESH
                 )
 
-    for side in (-1, 1, 0):
+    for side in (-1, 1, -2, 2, 0):
         toward(side, functools.partial(greet, side))
 
+    fetches = []
+
+    def fetch(src, dst):
+        copy = pltpu.make_async_copy(src, dst, local_sem.at[len(fetches)])
+        copy.start()
+        fetches.append(copy)
+        return copy
+
+    first_fetch = [fetch(single_hbm, single_ref), fetch(proj_hbm, proj_ref)]
     pair_fetch = [fetch(band_hbm, band_ref), fetch(pair_proj_hbm, pair_proj_ref)]
     id_fetch = [fetch(ids_hbm, ids_ref), fetch(starts_hbm, starts_ref)]
     atom_fetch = [fetch(atom_hbm, atom_ref)]
@@ -260,36 +261,75 @@
 
     near, far = pl.ds(0, HALF), pl.ds(HALF, HALF)
 
-    def close(slot, half):
+    def close(ds):
+        slot = ds + REACH
         id_buf[slot, 0:1] = jnp.full((1, ATOMS), -(2**20), jnp.int32)
         id_buf[slot, 1:2] = jnp.full((1, ATOMS), 2**20, jnp.int32)
         cond_buf[slot] = jnp.zeros(cond_buf.shape[1:], F32)
         pair_buf[slot] = jnp.zeros(pair_buf.shape[1:], BF16)
-        cot_buf[slot] = jnp.zeros(cot_buf.shape[1:], BF16)
-        halo_buf[half] = jnp.zeros((HALF, CA), BF16)
-        for at in (ATOMS, EXT):
-            other = (half.start + at - ATOMS) % ATOMS
-            rows_buf[at + other : at + other + HALF] = jnp.zeros((HALF, CA), BF16)
-        stream_buf[1, half] = jnp.zeros((HALF, CA), F32)
-        side = 1 if slot == 0 else 0
-        for back in range(2):
-            edge_recv[back, side] = jnp.zeros((CA, ATOMS), BF16)
-        sums_recv[side] = jnp.zeros((TOK, ACT), BF16)
-
-    pl.when(seq == 0)(lambda: close(0, far))
-    pl.when(seq == seqs - 1)(lambda: close(2, near))
+        if abs(ds) == REACH:
+            halo_buf[near if ds > 0 else far] = jnp.zeros((HALF, CA), BF16)
+        else:
+            side = (1 - ds) // 2
+            atom_buf[side] = jnp.zeros((ATOMS, CA), BF16)
+            cot_buf[1 + ds] = jnp.zeros(cot_buf.shape[1:], BF16)
+            for back in range(2):
+                edge_recv[back, side] = jnp.zeros((CA, ATOMS), BF16)
+            sums_recv[side] = jnp.zeros((TOK, ACT), BF16)
+
+    for ds in (-2, -1, 1, 2):
+        pl.when(jnp.logical_not(has[ds]))(functools.partial(close, ds))
 
     for copy in first_fetch:
         copy.wait()
-    cond_buf[1, 0] = nn(single_ref[...], proj_ref[...])
+    cond_buf[REACH, 0] = nn(single_ref[...], proj_ref[...])
     for copy in id_fetch:
         copy.wait()
     lane = iota((1, ATOMS), 1)
     own_first = jnp.zeros((1, ATOMS), jnp.int32)
     for b in range(ATOMS // QB):
         own_first = jnp.where(lane // QB == b, starts_ref[b], own_first)
-    id_buf[1, 0:1] = ids_ref[...]
-    id_buf[1, 1:2] = own_first
+    id_buf[REACH, 0:1] = ids_ref[...]
+    id_buf[REACH, 1:2] = own_first
+    places = sum(here.astype(jnp.int32) for here in has.values())
+    pl.semaphore_wait(barrier, 3 + 4 * places)
+
+    def outward(reach):
+        group = [
+            (cond_buf.at[REACH, 0], cond_buf.at[REACH - ds, dr], ds, dr, dc)
+            for ds, dr, dc in COND_PARTNERS
+            if abs(ds) in reach
+        ]
+        group += [
+            (id_buf.at[REACH], id_buf.at[REACH - ds], ds, 0, 0)
+            for ds in (-1, 1, -2, 2)
+            if abs(ds) in reach
+        ]
+        if REACH in reach:
+            group += [
+                (atom_hbm.at[near], halo_buf.at[near], -2, 0, 0),
+                (atom_hbm.at[far], halo_buf.at[far], 2, 0, 0),
+            ]
+        else:
+            group += [(atom_hbm, atom_buf.at[(ds + 1) // 2], ds, 0, 0) for ds in SIDES]
+        return send_all(group)
+
+    def outward_pairs(reach):
+        return send_all(
+            [
+                (
+                    pair_buf.at[REACH, pair_rows, pair_lanes],
+                    pair_buf.at[REACH - ds, pair_rows, pair_lanes],
+                    ds,
+                    dr,
+                    dc,
+                )
+                for ds, dr, dc in PARTNERS
+                if abs(ds) in reach
+            ]
+        )
+
+    cond_copies = outward((0, 1))
     for copy in pair_fetch:
         copy.wait()
     place_h = (iota((LAYERS * HEADS, CA), 1) == 8 * iota((LAYERS * HEADS, CA), 0)).astype(BF16)
@@ -307,36 +347,11 @@
     tile = jnp.concatenate([tile, jnp.zeros((PAIR_PAD - PAIR_COLS, CA), F32)], axis=0)
     pair_rows = pl.ds(pl.multiple_of(col * PAIR_PAD, 16), PAIR_PAD)
     pair_lanes = pl.ds(pl.multiple_of(row * CA, CA), CA)
-    pair_buf[1, pair_rows, pair_lanes] = tile.astype(BF16)
-
-    beyond = len(PARTNERS) // 3 + 1
-    pl.semaphore_wait(
-        barrier, beyond - 1 + beyond * (has[-1].astype(jnp.int32) + has[1].astype(jnp.int32))
-    )
-
-    cond_copies = send_all(
-        [
-            (cond_buf.at[1, 0], cond_buf.at[1 - ds, dr], ds, dr, dc)
-            for ds, dr, dc in COND_PARTNERS
-        ]
-        + [(id_buf.at[1], id_buf.at[1 - ds], ds, 0, 0) for ds in SIDES]
-        + [
-            (atom_hbm.at[near], halo_buf.at[near], -1, 0, 0),
-            (atom_hbm.at[far], halo_buf.at[far], 1, 0, 0),
-        ]
-    )
-    pair_copies = send_all(
-        [
-            (
-                pair_buf.at[1, pair_rows, pair_lanes],
-                pair_buf.at[1 - ds, pair_rows, pair_lanes],
-                ds,
-                dr,
-                dc,
-            )
-            for ds, dr, dc in PARTNERS
-        ]
-    )
+    pair_buf[REACH, pair_rows, pair_lanes] = tile.astype(BF16)
+
+    pair_copies = outward_pairs((0, 1))
+    far_copies = outward((2,)) + outward_pairs((2,))
+
     for copy in atom_fetch + weight_fetch:
         copy.wait()
     for n in range(LAYERS):
@@ -358,25 +373,32 @@
     atom_t = flip(atom_ref[...]).astype(F32)
 
     arrive(cond_copies)
-    left_ids = id_buf[0, 0:1] - token_base
-    right_ids = id_buf[2, 0:1] - token_base
-    halo_ids = jnp.where(low, right_ids, left_ids)
+    ids_at = {ds: id_buf[REACH + ds, 0:1] - token_base for ds in (-1, 0, 1)}
+    halo_ids = jnp.where(low, ids_at[1], ids_at[-1])
     halo_id_cols = as_cols(halo_ids)
+
+    def conditioning(slots):
+        cond = (cond_buf[slots, 0] + cond_buf[slots, 1]).astype(BF16).reshape(-1, CA)
+        return flip(cond)
+
     pick_ext = (iota((SPAN, EXT), 0) == jnp.concatenate([own_ids, halo_ids], axis=1)).astype(
         F32
     ).astype(BF16)
+    beside_atoms = [flip(atom_buf[side]).astype(F32) for side in range(2)]
+    stream_ext = jnp.concatenate([atom_t, jnp.where(low, *beside_atoms)], axis=1) + nn(
+        conditioning(slice(1, 4)), pick_ext
+    )
     pick = pick_ext[:, :ATOMS]
-    cond = (cond_buf[:, 0] + cond_buf[:, 1]).astype(BF16).reshape(SPAN, CA)
-    cond_t = flip(cond)
-    stream_ext = jnp.concatenate([atom_t, flip(halo_buf[...]).astype(F32)], axis=1) + nn(
-        cond_t, pick_ext
-    )
 
     position = iota((EXT, ATOMS), 0)
     position = jnp.where(position < ATOMS + HALF, position, position - EXT)
-    first = own_first - atom_base
-    outside = jnp.where((position >= first) & (position < first + KW), 0.0, -1e30)
-    outside = jnp.concatenate([outside] * HEADS, axis=1)
+
+    def mask_of(tile):
+        first = id_buf[REACH + tile, 1:2] - atom_base - tile * ATOMS
+        out = jnp.where((position >= first) & (position < first + KW), 0.0, -1e30)
+        return jnp.concatenate([out] * HEADS, axis=1)
+
+    outside = mask_of(0)
 
     place = iota((2 * CA, ATOMS), 0)
     head_of = (place // PAIR_ROWS) % HEADS
@@ -397,13 +419,13 @@
             axis=1,
         )
 
-    def table_of(n):
+    def table_of(n, tile):
         part = PAIR_ROWS * HEADS
         none = jnp.zeros((CA, CA), BF16)
         blocks = []
         for s in range(3):
             at = 2 * part * (s % 2)
-            here = pair_buf[s].astype(F32)
+            here = pair_buf[REACH - 1 + tile + s].astype(F32)
             halves = []
             for r in range(2):
                 shift = (at + part * r - part * n) % CA
@@ -425,8 +447,8 @@
             [(hit & (head_of == h)).astype(F32).astype(BF16) for h in range(HEADS)], axis=1
         )
 
-    def bias_of(taken, n, picks):
-        return nn(nn(taken, table_of(n)).astype(BF16), picks)
+    def bias_of(taken, n, tile, picks):
+        return nn(nn(taken, table_of(n, tile)).astype(BF16), picks)
 
     def right_rows(values):
         return jnp.concatenate(
@@ -440,16 +462,13 @@
 
     low_all = jnp.concatenate([low] * HEADS, axis=1)
 
-    def attend_own(n, kv_n, heads):
-        scores = nn(kv_n[:EXT, :CA], heads) * SCALE + bias[n]
+    def attend(kv_n, heads, bias_n):
+        scores = nn(kv_n[:EXT, :CA], heads) * SCALE + bias_n
         values_t = flip(kv_n[:EXT, CA:])
         exps = jnp.exp(scores - jnp.max(scores, axis=0, keepdims=True))
         weights = exps * (1.0 / jnp.sum(exps, axis=0, keepdims=True))
         rounded = weights.astype(BF16)
-        soft[n] = weights
-        soft_b[n] = rounded
-        key_t[n] = flip(kv_n[:EXT, :CA])
-        return jnp.concatenate(
+        attended = jnp.concatenate(
             [
                 nn(
                     values_t[width * h : width * (h + 1)],
@@ -459,6 +478,14 @@
             ],
             axis=0,
         )
+        return attended, weights, rounded
+
+    def attend_own(n, kv_n, heads):
+        attended, weights, rounded = attend(kv_n, heads, bias[n])
+        soft[n] = weights
+        soft_b[n] = rounded
+        key_t[n] = flip(kv_n[:EXT, :CA])
+        return attended
 
     def attend_rim(n, kv_n, heads):
         right_kv = right_rows(kv_n)
@@ -491,19 +518,20 @@
 
     def transition(n, stream, gates, attended, lanes):
         gated = gates * attended
-        gating[n, :, :lanes] = gates
-        gate_back[n] = gated[:, :ATOMS] * (1.0 - gates[:, :ATOMS])
         x_mid = stream + nn(out_t[n], gated.astype(BF16))
         normal, scaling = norm_rows(x_mid)
-        normal_m[n, :, :lanes] = normal
-        scale_m[n, :, :lanes] = scaling
         widened = nn(in_t[n], normal.astype(BF16))
         part_a = widened[:FFA]
         part_b = widened[FFA:]
         sig = jax.nn.sigmoid(part_a)
         act = part_a * sig
-        silu_a[n, :, :lanes] = act
-        back_a[n, :, :lanes] = part_b * (sig * (1.0 + part_a * (1.0 - sig)))
+        if lanes:
+            gating[n, :, :lanes] = gates
+            gate_back[n] = gated[:, :ATOMS] * (1.0 - gates[:, :ATOMS])
+            normal_m[n, :, :lanes] = normal
+            scale_m[n, :, :lanes] = scaling
+            silu_a[n, :, :lanes] = act
+            back_a[n, :, :lanes] = part_b * (sig * (1.0 + part_a * (1.0 - sig)))
         return x_mid + nn(down_t[n], (act * part_b).astype(BF16))
 
     def local_layer(n, stream_ext):
@@ -520,47 +548,29 @@
             own_picks[...] = bias_picks(own_ids)
             takes[:EXT] = take_of(jnp.concatenate([own_id_cols, halo_id_cols], axis=0))
             arrive(pair_copies)
-            bias[0] = bias_of(takes[:EXT], 0, own_picks[...]) + outside
+            bias[0] = bias_of(takes[:EXT], 0, 0, own_picks[...]) + outside
         attended = attend_own(n, kv[n // 2], heads)
         return transition(n, stream_ext[:, :ATOMS], gates, attended, ATOMS)
 
     stream = local_layer(0, stream_ext)
+    late_copies = send_all(
+        [(cot_hbm, cot_buf.at[1 - ds, dr], ds, dr, dc) for ds, dr, dc in COND_PARTNERS if abs(ds) < REACH]
+        + [(agg_hbm, agg_buf, 0, 1, 0)]
+    )
+
 
     normal, scaling = norm_rows(stream)
     normal_x[1, :, :ATOMS] = normal
     scale_x[1, :, :ATOMS] = scaling
-    rows_buf[:ATOMS] = flip(normal.astype(BF16))
-    lower, upper = near, far
-    inner_copies = send_all(
-        [
-            (rows_buf.at[lower], rows_buf.at[pl.ds(ATOMS, HALF)], -1, 0, 0),
-            (rows_buf.at[upper], rows_buf.at[pl.ds(ATOMS + HALF, HALF)], 1, 0, 0),
-        ]
-    )
-    outer_copies = send_all(
-        [
-            (rows_buf.at[upper], rows_buf.at[pl.ds(EXT, HALF)], -1, 0, 0),
-            (rows_buf.at[lower], rows_buf.at[pl.ds(EXT + HALF, HALF)], 1, 0, 0),
-        ]
-    )
-    stream_buf[0] = flip(stream)
-    stream_copies = send_all(
-        [
-            (stream_buf.at[0, lower], stream_buf.at[1, lower], -1, 0, 0),
-            (stream_buf.at[0, upper], stream_buf.at[1, upper], 1, 0, 0),
-        ]
-    )
-    late_copies = send_all(
-        [(cot_hbm, cot_buf.at[1 - ds, dr], ds, dr, dc) for ds, dr, dc in COND_PARTNERS]
-        + [(agg_hbm, agg_buf, 0, 1, 0)]
-    )
-
-    kv_wide[:ATOMS] = nn(rows_buf[:ATOMS], attn_in_ref[1, :, CA : 3 * CA]).astype(BF16)
-    heads = by_head(nn(query_t[1], normal.astype(BF16)).astype(BF16))
-    q_heads[1] = flip(heads)
-    outer_ids = pltpu.roll(jnp.where(low, left_ids, right_ids), HALF, 1)
+    normed = normal.astype(BF16)
+    rows_own = flip(normed)
+    kv_wide[:ATOMS] = nn(rows_own, attn_in_ref[1, :, CA : 3 * CA]).astype(BF16)
+    own_heads = by_head(nn(query_t[1], normed).astype(BF16))
+    q_heads[1] = flip(own_heads)
+    own_gates = jax.nn.sigmoid(nn(gate_t[1], normed))
+    outer_ids = pltpu.roll(jnp.where(low, ids_at[-1], ids_at[1]), HALF, 1)
     takes[EXT:] = take_of(as_cols(outer_ids))
-    mixed = nn(takes[...], table_of(1)).astype(BF16)
+    mixed = nn(takes[...], table_of(1, 0)).astype(BF16)
     bias[1] = nn(mixed[:EXT], own_picks[...]) + outside
     rim_full = nn(mixed, bias_picks(halo_ids))
     rim_rows = iota((3 * HALF, ATOMS), 0)
@@ -570,30 +580,71 @@
         jnp.where(rim_rows < ATOMS, rim_rows - ATOMS, rim_rows - EXT),
     )
     rim_position = jnp.where(low, HALF + rim_rows, left_position)
-    rim_first = jnp.where(low, id_buf[2, 1:2], id_buf[0, 1:2]) - atom_base
+    rim_first = jnp.where(low, id_buf[REACH + 1, 1:2], id_buf[REACH - 1, 1:2]) - atom_base
     rim_outside = jnp.where(
         (rim_position >= rim_first) & (rim_position < rim_first + KW), 0.0, -1e30
     )
     bias_rim[...] = jnp.where(low_all, right_rows(rim_full), left_rows(rim_full)) + jnp.concatenate(
         [rim_outside] * HEADS, axis=1
     )
-    bias[2] = bias_of(takes[:EXT], 2, own_picks[...]) + outside
+    bias[2] = bias_of(takes[:EXT], 2, 0, own_picks[...]) + outside
     at_token = jnp.concatenate([own_id_cols, halo_id_cols], axis=0) == iota((EXT, CA), 1)
     pick_t = at_token[:ATOMS].astype(F32).astype(BF16)[:, :SPAN]
     token_atoms = jnp.sum(at_token.astype(F32), axis=0, keepdims=True)
     atom_counts = jnp.sum(jnp.where(at_token[:ATOMS], token_atoms, 0.0), axis=1, keepdims=True)
     inverse = 1.0 / jnp.maximum(atom_counts, 1.0)
-    arrive(inner_copies)
-    kv_wide[ATOMS:EXT] = nn(rows_buf[ATOMS:EXT], attn_in_ref[1, :, CA : 3 * CA]).astype(BF16)
-    attended = attend_own(1, kv_wide, heads)
-    gates = jax.nn.sigmoid(nt(gate_t[1], rows_buf[:EXT]))
-    heads = by_head(nt(query_t[1], rows_buf[ATOMS:EXT]).astype(BF16))
-    q_rim[...] = flip(heads)
-    arrive(outer_copies)
-    kv_wide[EXT:] = nn(rows_buf[EXT:], attn_in_ref[1, :, CA : 3 * CA]).astype(BF16)
-    attended = jnp.concatenate([attended, attend_rim(1, kv_wide, heads)], axis=1)
-    arrive(stream_copies)
-    stream_ext = jnp.concatenate([stream, flip(stream_buf[1])], axis=1)
+
+    arrive(far_copies)
+    ids_at.update({ds: id_buf[REACH + ds, 0:1] - token_base for ds in (-2, 2)})
+    side_ids = jnp.concatenate(
+        [ids_at[1], ids_at[-1], jnp.where(low, ids_at[2], ids_at[-2])], axis=1
+    )
+    pick_side = (iota((SLOTS * TOK, 3 * ATOMS), 0) - TOK == side_ids).astype(F32).astype(BF16)
+    stream_side = jnp.concatenate(beside_atoms + [flip(halo_buf[...]).astype(F32)], axis=1) + nn(
+        conditioning(slice(0, SLOTS)), pick_side
+    )
+    normal_side, _ = norm_rows(stream_side)
+    normed_side = normal_side.astype(BF16)
+    rows_side = flip(normed_side)
+    kv_side[...] = nn(rows_side, attn_in_ref[0, :, CA : 3 * CA]).astype(BF16)
+    queries = nn(query_t[0], normed_side[:, :EXT]).astype(BF16)
+    gates = jax.nn.sigmoid(nn(gate_t[0], normed_side[:, :EXT]))
+    kv_of = {
+        1: [kv_side[:ATOMS], kv_side[EXT : EXT + HALF], kv[0, HALF:ATOMS]],
+        -1: [kv_side[ATOMS:EXT], kv[0, :HALF], kv_side[EXT + HALF :]],
+    }
+    attended = []
+    for place, tile in enumerate((1, -1)):
+        here = ids_at[tile] - TOK * tile
+        there = jnp.where(low, ids_at[tile + 1], ids_at[tile - 1]) - TOK * tile
+        taken = take_of(jnp.concatenate([as_cols(here), as_cols(there)], axis=0))
+        bias_here = bias_of(taken, 0, tile, bias_picks(here)) + mask_of(tile)
+        attended.append(
+            attend(
+                jnp.concatenate(kv_of[tile], axis=0),
+                by_head(queries[:, ATOMS * place : ATOMS * (place + 1)]),
+                bias_here,
+            )[0]
+        )
+    stream_side = transition(
+        0, stream_side[:, :EXT], gates, jnp.concatenate(attended, axis=1), 0
+    )
+
+    rows_side = flip(norm_rows(stream_side)[0].astype(BF16))
+    rows_right, rows_left = rows_side[:ATOMS], rows_side[ATOMS:]
+    rows_side = jnp.concatenate(
+        [rows_right[:HALF], rows_left[HALF:], rows_right[HALF:], rows_left[:HALF]], axis=0
+    )
+    kv_wide[ATOMS:] = nn(rows_side, attn_in_ref[1, :, CA : 3 * CA]).astype(BF16)
+    rim_heads = by_head(nt(query_t[1], rows_side[:ATOMS]).astype(BF16))
+    q_rim[...] = flip(rim_heads)
+    gates = jnp.concatenate(
+        [own_gates, jax.nn.sigmoid(nt(gate_t[1], rows_side[:ATOMS]))], axis=1
+    )
+    attended = jnp.concatenate([attend_own(1, kv_wide, own_heads), attend_rim(1, kv_wide, rim_heads)], axis=1)
+    stream_ext = jnp.concatenate(
+        [stream, jnp.where(low, stream_side[:, :ATOMS], stream_side[:, ATOMS:])], axis=1
+    )
     stream_ext = transition(1, stream_ext, gates, attended, EXT)
 
     stream = local_layer(2, stream_ext)
@@ -756,11 +807,11 @@
     d_cond = per_token(pick_ext[TOK : 2 * TOK], gradient)
     high, rest = split(d_cond)
     single_out[...] = (nt(high, proj_ref[...]) + nt(rest, proj_ref[...])).astype(BF16)
-    for side in (0, -1, 1):
+    for side in (0, -1, 1, -2, 2):
         each(copies, side, side, lambda copy: copy.wait_send())
 
 
-N_COPIES = 5 + 2 + 2 + 11 + 5 + 1 + 6 + 2 + 2 + 2
+N_COPIES = 9 + 4 + 4 + 19 + 5 + 1 + 2 + 2 + 2
 
 
 def hand_on(act, grad, single, act_out, grad_out, single_out):
@@ -815,14 +866,14 @@
             scratch(BF16, LAYERS, CA, 2 * FFA),
             scratch(BF16, LAYERS, FFA, CA),
             scratch(BF16, CA, ACT),
-            scratch(jnp.int32, 3, 2, ATOMS),
+            scratch(jnp.int32, SLOTS, 2, ATOMS),
             scratch(BF16, ATOMS, CA),
-            scratch(F32, 3, 2, TOK, CA),
-            scratch(BF16, 3, 2 * PAIR_PAD, 2 * CA),
+            scratch(F32, SLOTS, 2, TOK, CA),
+            scratch(BF16, SLOTS, 2 * PAIR_PAD, 2 * CA),
             scratch(BF16, 3, 2, TOK, ACT),
             scratch(BF16, CA, ACT),
-            scratch(BF16, 3 * ATOMS, CA),
-            scratch(F32, 2, ATOMS, CA),
+            scratch(BF16, 2, ATOMS, CA),
+            scratch(BF16, 3 * ATOMS, 2 * CA),
             scratch(BF16, 2, EXT, 2 * CA),
             scratch(BF16, 3 * ATOMS, 2 * CA),
             scratch(F32, LAYERS, EXT, ALL),

time: 39 us -> 38.7 us (level)
  Pallas kernels: 38.2 us -> 37.8 us
where the time goes in v4:
time: 38.7 us; the launch traced here: 38.5 us
  Pallas kernels  37.8 us (98%)
  between operations  0.64 us (2%)
    pallas_call x1, Pallas kernels, local(): pl.pallas_call(kernel, out_shape=results, in_specs=[hbm] * 14, out_specs=...  36.5 us
    pallas_call x1, Pallas kernels, local(): pl.pallas_call(hand_on, out_shape=results, in_specs=[vmem] * 3, out_specs...  1.38 us

profile of v4, /device:TPU:384, one launch (start us, length us, event | category | flops | bytes accessed | tf_op | source)
XLA Modules:
  0.0 38.5 jit_solution(328017409290533452)
XLA Ops:
  0.6 36.5 %atoms.1 = (bf16[16,384]{1,0:T(8,128)(2,1)}, bf16[128,128]{1,0:T(8,128)(2,1)}, bf16[16,192]{1,0:T(8,128)(2,1)}) custom-call(bf16[128,128]{1,0:T(8,128)(2,1)} %atom_hbm.1, bf16[16,192]{1,0:T(8,128)(2,1)} %single_hbm.1, bf16[8,40,128]{2,1,0:T(8,128)(2,1)} %band_hbm.1, s32[1,16]{1,0:T(1,128)} %bitcast.4, s32[1,128]{1,0:T(1,128)} %bitcast.5, s32[4]{0:T(128)} %starts_hbm.1, ...), custom_call_target="tpu_custom_call" | custom-call | flops 2000000000 | bytes 2000000 | tf_op jit(solution)/shard_map/atoms/pallas_call | solution.py:850
  37.1 1.4 %results.1 = (bf16[16,384]{1,0:T(8,128)(2,1)}, bf16[128,128]{1,0:T(8,128)(2,1)}, bf16[16,192]{1,0:T(8,128)(2,1)}) custom-call(bf16[16,384]{1,0:T(8,128)(2,1)} %get-tuple-element.6.act, bf16[128,128]{1,0:T(8,128)(2,1)} %get-tuple-element.7.grad, bf16[16,192]{1,0:T(8,128)(2,1)} %get-tuple-element.8.single), custom_call_target="tpu_custom_call" | custom-call | tf_op jit(solution)/shard_map/results/pallas_call | solution.py:934

commit v5 on v4

--- a/solution.py
+++ b/solution.py
@@ -167,6 +167,7 @@
     sums_send,
     sums_recv,
     local_sem,
+    relay_sem,
     send_sem,
     recv_sem,
 ):
@@ -234,7 +235,7 @@
                     barrier, inc=1, device_id=partner(ds, dr, dc), device_id_type=MESH
                 )
 
-    for side in (-1, 1, -2, 2, 0):
+    for side in (-1, 1, 0):
         toward(side, functools.partial(greet, side))
 
     fetches = []
@@ -291,8 +292,19 @@
         own_first = jnp.where(lane // QB == b, starts_ref[b], own_first)
     id_buf[REACH, 0:1] = ids_ref[...]
     id_buf[REACH, 1:2] = own_first
-    places = sum(here.astype(jnp.int32) for here in has.values())
+    places = has[-1].astype(jnp.int32) + has[1].astype(jnp.int32)
     pl.semaphore_wait(barrier, 3 + 4 * places)
+
+    def tell():
+        for ds in SIDES:
+            pl.semaphore_signal(
+                relay_sem.at[(ds + 1) // 2],
+                inc=1,
+                device_id=partner(ds, 0, 0),
+                device_id_type=MESH,
+            )
+
+    pl.when(jnp.logical_and(has[-1], has[1]))(tell)
 
     def outward(reach):
         group = [
@@ -350,6 +362,8 @@
     pair_buf[REACH, pair_rows, pair_lanes] = tile.astype(BF16)
 
     pair_copies = outward_pairs((0, 1))
+    for ds in (-2, 2):
+        toward(ds, functools.partial(pl.semaphore_wait, relay_sem.at[(2 - ds) // 4], 1))
     far_copies = outward((2,)) + outward_pairs((2,))
 
     for copy in atom_fetch + weight_fetch:
@@ -905,6 +919,7 @@
             scratch(BF16, 2, TOK, ACT),
             scratch(BF16, 2, TOK, ACT),
             pltpu.SemaphoreType.DMA((14,)),
+            pltpu.SemaphoreType.REGULAR((2,)),
             pltpu.SemaphoreType.DMA((N_COPIES,)),
             pltpu.SemaphoreType.DMA((N_COPIES,)),
         ],

time: 38.7 us -> 38.3 us (0.990)
  no operation moved by 1% of the time
where the time goes in v5:
time: 38.3 us; the launch traced here: 38.1 us
  Pallas kernels  37.5 us (98%)
  between operations  0.64 us (2%)
    pallas_call x1, Pallas kernels, local(): pl.pallas_call(kernel, out_shape=results, in_specs=[hbm] * 14, out_specs=...  36.1 us
    pallas_call x1, Pallas kernels, local(): pl.pallas_call(hand_on, out_shape=results, in_specs=[vmem] * 3, out_specs...  1.38 us

profile of v5, /device:TPU:384, one launch (start us, length us, event | category | flops | bytes accessed | tf_op | source)
XLA Modules:
  0.0 38.1 jit_solution(15265563008484543314)
XLA Ops:
  0.6 36.1 %atoms.1 = (bf16[16,384]{1,0:T(8,128)(2,1)}, bf16[128,128]{1,0:T(8,128)(2,1)}, bf16[16,192]{1,0:T(8,128)(2,1)}) custom-call(bf16[128,128]{1,0:T(8,128)(2,1)} %atom_hbm.1, bf16[16,192]{1,0:T(8,128)(2,1)} %single_hbm.1, bf16[8,40,128]{2,1,0:T(8,128)(2,1)} %band_hbm.1, s32[1,16]{1,0:T(1,128)} %bitcast.4, s32[1,128]{1,0:T(1,128)} %bitcast.5, s32[4]{0:T(128)} %starts_hbm.1, ...), custom_call_target="tpu_custom_call" | custom-call | flops 2000000000 | bytes 2000000 | tf_op jit(solution)/shard_map/atoms/pallas_call | solution.py:864
  36.8 1.4 %results.1 = (bf16[16,384]{1,0:T(8,128)(2,1)}, bf16[128,128]{1,0:T(8,128)(2,1)}, bf16[16,192]{1,0:T(8,128)(2,1)}) custom-call(bf16[16,384]{1,0:T(8,128)(2,1)} %get-tuple-element.6.act, bf16[128,128]{1,0:T(8,128)(2,1)} %get-tuple-element.7.grad, bf16[16,192]{1,0:T(8,128)(2,1)} %get-tuple-element.8.single), custom_call_target="tpu_custom_call" | custom-call | tf_op jit(solution)/shard_map/results/pallas_call | solution.py:949
